TPU v7x, 128 devices: a whole 4x4x4 slice. The times are simulated.
128 devices in a mesh: tm: 4 (over y_hi, core), chan: 32 (over y_lo, x, z).
Axes of the slice: x: 4, y: 4 (y_hi: 2, y_lo: 2; y = y_hi * 2 + y_lo), z: 4, core: 2. Of those that a mesh axis runs over, the one named last changes fastest.
Arguments:
- samples: bfloat16 [2048, 262144], P('chan', 'tm'), may hold values from -6 to 6
- tap_weights: float32 [16, 2048], replicated, may hold values from -1.5 to 1.5
Outputs:
- visibilities: bfloat16 [128, 2, 2048, 2048], P('chan', None, 'tm')
All inputs are finite; a program needn't handle non-finite values.
Results may differ from a plain program's by a relative error of at most 0.012.
Values may be sent and summed in bfloat16 or wider, within the bound.
No kernel may reach another device: no remote copies, remote signals or barrier semaphores. Data moves between devices by JAX's collectives and lax.ppermute only.
A program may use at most 320 MiB of HBM per device.

v0:
```python
import math

import jax
import jax.numpy as jnp
from jax import lax
from jax.sharding import PartitionSpec as P

NFFT = 2048
TAPS = 16
CH0 = 256
CH_DEV = 4


def from_behind(value, axis, steps):
    count = lax.axis_size(axis)
    leading, last = (max(0, -steps), min(count, count - steps))
    return lax.ppermute(value, axis, [(source, source + steps) for source in range(leading, last)])


def channel_rows(groups):
    row_count = groups * CH_DEV * 2
    row_index = jnp.arange(row_count, dtype=jnp.int32)
    channel = CH0 + row_index // 2
    sample = jnp.arange(NFFT, dtype=jnp.int32)
    phase_index = channel[:, None] * sample[None, :] % NFFT
    angle_rad = phase_index.astype(jnp.float32) * (2.0 * math.pi / NFFT)
    norm_scale = 1.0 / math.sqrt(NFFT)
    return jnp.where(
        (row_index % 2 == 0)[:, None],
        jnp.cos(angle_rad) * norm_scale,
        -jnp.sin(angle_rad) * norm_scale,
    )


def filter_frames(extended, tap_weights, frame_count):
    summed = jnp.zeros((extended.shape[0], frame_count, extended.shape[2]), jnp.float32)
    for tap_index in range(TAPS):
        summed = (
            summed
            + extended[:, tap_index : tap_index + frame_count].astype(jnp.float32)
            * tap_weights[tap_index]
        )
    return summed


def project(filtered, dft_rows, groups):
    signal_count, frame_count, width_fft = filtered.shape
    flat_rows = filtered.reshape(signal_count * frame_count, width_fft)
    spectrum = lax.dot_general(
        dft_rows,
        flat_rows,
        (((1,), (1,)), ((), ())),
        precision=lax.Precision.HIGHEST,
        preferred_element_type=jnp.float32,
    )
    return spectrum.reshape(groups, CH_DEV, 2, signal_count, frame_count)


def to_columns(block, signal_count):
    time_count, source_count, chan_count, parts_count, width_all = block.shape
    frame_count = width_all // signal_count
    split_block = block.reshape(
        time_count, source_count, chan_count, parts_count, signal_count, frame_count
    )
    turned_block = jnp.transpose(split_block, (2, 3, 0, 5, 1, 4))
    return turned_block.reshape(
        chan_count, parts_count * time_count * frame_count, source_count * signal_count
    )


def correlate(columns, first_row, row_count):
    half_count = columns.shape[1] // 2
    left_rows = lax.dynamic_slice_in_dim(columns, first_row, row_count, 2)
    turned = jnp.concatenate([left_rows[:, half_count:], -left_rows[:, :half_count]], axis=1)
    dims = (((1,), (1,)), ((0,), (0,)))
    power_sum = lax.dot_general(left_rows, columns, dims, preferred_element_type=jnp.float32)
    cross_sum = lax.dot_general(turned, columns, dims, preferred_element_type=jnp.float32)
    return jnp.stack([power_sum, cross_sum], axis=1)


def per_device(samples, tap_weights):
    parts_tm = lax.axis_size("tm")
    parts_chan = lax.axis_size("chan")
    signal_count, width_dev = samples.shape
    frame_count = width_dev // NFFT
    blocks = samples.reshape(signal_count, frame_count, NFFT)
    tail_frames = blocks[:, frame_count - (TAPS - 1) :]
    dft_rows = channel_rows(parts_chan)
    prior_tail = from_behind(tail_frames, "tm", 1)
    extended = jnp.concatenate([prior_tail, blocks], axis=1)
    voltages = project(
        filter_frames(extended, tap_weights, frame_count), dft_rows, parts_chan
    ).astype(jnp.bfloat16)
    flat_volts = voltages.reshape(parts_chan, CH_DEV, 2, signal_count * frame_count)
    row_count = parts_chan // parts_tm * signal_count
    first_row = lax.axis_index("tm") * row_count
    outgoing = jnp.broadcast_to(flat_volts[None], (parts_tm,) + flat_volts.shape)
    outgoing = outgoing.reshape((parts_tm * parts_chan,) + flat_volts.shape[1:])
    incoming = lax.all_to_all(outgoing, ("tm", "chan"), split_axis=0, concat_axis=0, tiled=True)
    incoming = incoming.reshape((parts_tm, parts_chan) + flat_volts.shape[1:])
    summed = correlate(to_columns(incoming, signal_count), first_row, row_count)
    return (summed * (1.0 / (frame_count * parts_tm))).astype(jnp.bfloat16)


def solution(mesh):
    return jax.shard_map(
        per_device,
        mesh=mesh,
        in_specs=(P("chan", "tm"), P()),
        out_specs=P("chan", None, "tm", None),
        check_vma=False,
    )
```

profile of v0, /device:TPU:1, one launch (start us, length us, event | category | flops | bytes accessed | tf_op | source)
XLA Modules:
  0.0 317.3 jit_solution(4909178290704733314)
XLA Ops:
  0.0 0.0 copy-start.1
  0.0 8.5 %copy.43 = bf16[8,32,8,2048]{3,2,0,1:T(8,128)(2,1)} copy(bf16[8,32,8,2048]{3,2,1,0:T(8,128)(2,1)} %bitcast.67) | data formatting | bytes 16777216 | tf_op jit(solution)/shard_map/reshape | solution.py:86
  8.5 2.4 slice.136
  10.9 6.2 %collective-permute-start = (bf16[64,15,2048]{2,0,1:T(8,128)(2,1)S(1)}, bf16[64,15,2048]{2,0,1:T(8,128)(2,1)S(1)}, u32[]{:S(2)}, u32[]{:S(2)}) collective-permute-start(bf16[64,15,2048]{2,0,1:T(8,128)(2,1)S(1)} %slice.136), channel_id=1, source_target_pairs={{0,32},{32,64},{64,96},{1,33},{33,65},{65,97},{2,34},{34,66},{66,9... | collective-permute-start | bytes 11796488 | tf_op jit(solution)/shard_map/ppermute | solution.py:17
  17.1 0.0 copy-done.1
  17.2 0.1 fusion.122
  17.3 8.6 %fusion.131 = f32[32,4,2,2048,1]{3,0,4,2,1:T(8,128)S(1)} fusion(s32[32,4,2]{0,2,1:T(2,128)S(1)} %fusion.113, pred[32,4,2]{0,2,1:T(4,128)(4,1)S(1)} %fusion.114), kind=kLoop, calls=%fused_computation.91.clone.clone.clone.2 | loop fusion | flops 9437184 | bytes 2098432 | tf_op jit(solution)/shard_map/dot_general | solution.py:49
  25.8 33.9 %collective-permute-done = bf16[64,15,2048]{2,0,1:T(8,128)(2,1)S(1)} collective-permute-done((bf16[64,15,2048]{2,0,1:T(8,128)(2,1)S(1)}, bf16[64,15,2048]{2,0,1:T(8,128)(2,1)S(1)}, u32[]{:S(2)}, u32[]{:S(2)}) %collective-permute-start) | collective-permute-done | bytes 3932192 | tf_op jit(solution)/shard_map/ppermute | solution.py:17
  59.7 2.2 constant_dynamic-update-slice_fusion.1
  61.9 8.4 %constant_dynamic-update-slice_fusion = bf16[64,47,2048]{2,0,1:T(8,128)(2,1)} fusion(bf16[64,47,2048]{2,0,1:T(8,128)(2,1)} %constant_dynamic-update-slice_fusion.1, bf16[8,32,8,2048]{3,2,1,0:T(8,128)(2,1)} %bitcast.68), kind=kLoop, calls=%fused_computation.116 | loop fusion | bytes 16777216 | tf_op jit(solution)/shard_map/concatenate | solution.py:90
  70.4 67.0 %fusion.97 = bf16[32,4,2,64,32]{3,0,4,2,1:T(8,128)(2,1)S(1)} fusion(bf16[64,47,2048]{2,0,1:T(8,128)(2,1)} %constant_dynamic-update-slice_fusion, f32[2048]{0:T(1024)S(1)} %bitcast.86, f32[2048]{0:T(1024)S(1)} %bitcast.87, f32[2048]{0:T(1024)S(1)} %bitcast.73, f32[2048]{0:T(1024)S(1)} %bitcast.74, f32[2048]{0:T(1024)S(1)} %bitcast.75, ...), kind=kOutput, calls=%fused_computation.101 | convolution fusion | flops 13082558464 | bytes 137494528 | tf_op jit(solution)/shard_map/dot_general | solution.py:49
  137.4 3.6 %copy.31 = bf16[32,4,2,64,32]{4,3,2,1,0:T(8,128)(2,1)} copy(bf16[32,4,2,64,32]{3,0,4,2,1:T(8,128)(2,1)S(1)} %fusion.97) | data formatting | bytes 2097152 | tf_op jit(solution)/shard_map/broadcast_in_dim | solution.py:97
  141.0 6.5 %reshape.100 = bf16[32,4,2,2048]{3,2,1,0:T(2,128)(2,1)S(1)} reshape(bf16[32,4,2,64,32]{4,3,2,1,0:T(8,128)(2,1)} %copy.31) | data formatting | bytes 2097152 | tf_op jit(solution)/shard_map/broadcast_in_dim | solution.py:97
  147.5 6.4 %broadcast_in_dim.20 = bf16[4,32,4,2,2048]{4,3,2,1,0:T(2,128)(2,1)} broadcast(bf16[32,4,2,2048]{3,2,1,0:T(2,128)(2,1)S(1)} %reshape.100), dimensions={1,2,3,4} | broadcast | bytes 5242880 | tf_op jit(solution)/shard_map/broadcast_in_dim | solution.py:97
  153.9 11.6 %all-to-all-start = ((bf16[128,4,2,2048]{3,2,1,0:T(2,128)(2,1)}), bf16[128,4,2,2048]{3,2,1,0:T(2,128)(2,1)}, u32[]{:S(2)}, u32[]{:S(2)}) async-start(bf16[128,4,2,2048]{3,2,1,0:T(2,128)(2,1)} %bitcast.71), calls=%async_computation | async-start | bytes 8388608 | tf_op jit(solution)/shard_map/all_to_all | solution.py:99
  165.6 51.6 %all-to-all-done = bf16[128,4,2,2048]{3,2,1,0:T(2,128)(2,1)} async-done(((bf16[128,4,2,2048]{3,2,1,0:T(2,128)(2,1)}), bf16[128,4,2,2048]{3,2,1,0:T(2,128)(2,1)}, u32[]{:S(2)}, u32[]{:S(2)}) %all-to-all-start) | async-done | bytes 4194336 | tf_op jit(solution)/shard_map/all_to_all | solution.py:99
  217.2 6.5 %copy.22 = bf16[128,4,2,2048]{3,0,2,1:T(8,128)(2,1)} copy(bf16[128,4,2,2048]{3,2,1,0:T(2,128)(2,1)} %all-to-all-done) | data formatting | bytes 8388608 | tf_op jit(solution)/shard_map/all_to_all | solution.py:99
  223.7 19.4 %reshape_reshape.3 = bf16[4,32,4,2,64,32]{5,4,1,0,3,2:T(8,128)(2,1)} reshape(bf16[128,4,2,2048]{3,0,2,1:T(8,128)(2,1)} %copy.22) | data formatting | bytes 8388608 | tf_op jit(solution)/shard_map/reshape;reshape | solution.py:62
  243.1 19.0 %copy.23 = bf16[4,2,4,32,32,64]{5,4,3,2,1,0:T(8,128)(2,1)} copy(bf16[4,2,4,32,32,64]{3,5,4,2,1,0:T(8,128)(2,1)} %bitcast.66) | data formatting | bytes 8388608 | tf_op jit(solution)/shard_map/transpose | solution.py:65
  262.1 12.3 %reshape.97 = bf16[4,256,2048]{2,1,0:T(8,128)(2,1)} reshape(bf16[4,2,4,32,32,64]{5,4,3,2,1,0:T(8,128)(2,1)} %copy.23) | data formatting | bytes 8388608 | tf_op jit(solution)/shard_map/reshape | solution.py:66
  274.4 0.0 copy-start
  274.4 5.0 %convolution_bitcast_fusion.1 = f32[4,1,512,2048]{3,2,0,1:T(8,128)S(1)} fusion(bf16[4,256,2048]{2,1,0:T(8,128)(2,1)} %reshape.97, s32[]{:T(128)S(6)} %select_n.47), kind=kOutput, calls=%fused_computation.84 | convolution fusion | flops 2147483648 | bytes 22020100 | tf_op jit(solution)/shard_map/dot_general | solution.py:76
  279.4 0.0 copy-done
  279.4 0.2 constant_dynamic-slice_fusion
  279.6 8.6 %convolution_bitcast_fusion = f32[4,1,512,2048]{3,2,0,1:T(8,128)} fusion(bf16[4,256,2048]{2,1,0:T(8,128)(2,1)S(1)} %copy-done, bf16[4,128,512]{2,1,0:T(8,128)(2,1)S(1)} %get-tuple-element.6, bf16[4,128,512]{2,1,0:T(8,128)(2,1)S(1)} %get-tuple-element.5), kind=kOutput, calls=%fused_computation.83 | convolution fusion | flops 2149580800 | bytes 22020096 | tf_op jit(solution)/shard_map/dot_general | solution.py:77
  288.2 15.0 %fusion = bf16[4,2,512,2048]{3,2,0,1:T(8,128)(2,1)} fusion(f32[4,1,512,2048]{3,2,0,1:T(8,128)} %convolution_bitcast_fusion, f32[4,1,512,2048]{3,2,0,1:T(8,128)S(1)} %convolution_bitcast_fusion.1), kind=kLoop, calls=%fused_computation.1 | loop fusion | flops 25165824 | bytes 50331648 | tf_op jit(solution)/shard_map/convert_element_type | solution.py:102
  303.2 14.2 %copy.26 = bf16[4,2,512,2048]{3,2,1,0:T(8,128)(2,1)} copy(bf16[4,2,512,2048]{3,2,0,1:T(8,128)(2,1)} %fusion) | data formatting | bytes 33554432 | tf_op jit(solution)/shard_map/convert_element_type | solution.py:102
  (2 shorter events, 0.0 us)
Async XLA Ops:
  0.0 17.1 %copy-start.1 = (f32[16,2048]{1,0:T(8,128)S(1)}, f32[16,2048]{1,0:T(8,128)}, u32[]{:S(2)}) copy-start(f32[16,2048]{1,0:T(8,128)} %param.3) | copy-start | bytes 393220
  10.9 48.8 %collective-permute-start = (bf16[64,15,2048]{2,0,1:T(8,128)(2,1)S(1)}, bf16[64,15,2048]{2,0,1:T(8,128)(2,1)S(1)}, u32[]{:S(2)}, u32[]{:S(2)}) collective-permute-start(bf16[64,15,2048]{2,0,1:T(8,128)(2,1)S(1)} %slice.136), channel_id=1, source_target_pairs={{0,32},{32,64},{64,96},{1,33},{33,65},{65,97},{2,34},{34,66},{66,9... | collective-permute-start | bytes 11796488 | tf_op jit(solution)/shard_map/ppermute | solution.py:17
  153.9 63.3 %all-to-all-start = ((bf16[128,4,2,2048]{3,2,1,0:T(2,128)(2,1)}), bf16[128,4,2,2048]{3,2,1,0:T(2,128)(2,1)}, u32[]{:S(2)}, u32[]{:S(2)}) async-start(bf16[128,4,2,2048]{3,2,1,0:T(2,128)(2,1)} %bitcast.71), calls=%async_computation | async-start | bytes 8388608 | tf_op jit(solution)/shard_map/all_to_all | solution.py:99
  274.4 5.0 %copy-start = (bf16[4,256,2048]{2,1,0:T(8,128)(2,1)S(1)}, bf16[4,256,2048]{2,1,0:T(8,128)(2,1)}, u32[]{:S(2)}) copy-start(bf16[4,256,2048]{2,1,0:T(8,128)(2,1)} %reshape.97) | copy-start | bytes 12582916
where the time goes:
time: 319 us; the launch traced here: 317 us
  local copies, waits for them, and re-layouts  109 us (34%)
  waiting for transfers between devices  85.5 us (27%)
  matrix products  80.6 us (25%)
  other arithmetic  23.8 us (7%)
  starting transfers between devices  17.9 us (6%)
    dot_general x1, matrix products, project(): lax.dot_general(dft_rows, flat_rows, (((1,), (1,)), ((), ())), precision=...  67 us
    all_to_all x1, waiting for transfers between devices, per_device(): lax.all_to_all(outgoing, ('tm', 'chan'), split_axis=0, concat_axis=0, til...  51.6 us
    ppermute x1, waiting for transfers between devices, from_behind(): lax.ppermute(value, axis, [(source, source + steps) for source in range(l...  33.9 us
    another operation x1, local copies, waits for them, and re-layouts, to_columns(): block.reshape(time_count, source_count, chan_count, parts_count, signal_c...  19.4 us
    transpose x1, local copies, waits for them, and re-layouts, to_columns(): turned_block = jnp.transpose(split_block, (2, 3, 0, 5, 1, 4))  19 us
    broadcast_in_dim x3, local copies, waits for them, and re-layouts, per_device(): jnp.broadcast_to(flat_volts[None], (parts_tm,) + flat_volts.shape)  16.5 us
    convert_element_type x1, other arithmetic, per_device(): return (summed * (1.0 / (frame_count * parts_tm))).astype(jnp.bfloat16)  15 us
    convert_element_type x1, local copies, waits for them, and re-layouts, per_device(): return (summed * (1.0 / (frame_count * parts_tm))).astype(jnp.bfloat16)  14.2 us
  transfers between devices with their start and end apart: 2, of which 2 were waited for; matrix products, arithmetic and copies ran while one was open for 3% of the time, Pallas kernels for 0%

commit v1 on v0

v1 whole, which is shorter than its diff:
```python
import functools
import math

import jax
import jax.numpy as jnp
import numpy as np
from jax import lax
from jax.experimental import pallas as pl
from jax.experimental.pallas import tpu as pltpu
from jax.sharding import Mesh
from jax.sharding import PartitionSpec as P

NFFT = 2048
TAPS = 16
CH0 = 256
CH_DEV = 4
GROUPS = 32
COLS = GROUPS * CH_DEV * 2
SIG = 64
FRAMES = 32
HALF = 16
NT = 512
MIB = 2**20
PEERS = ("yh", "yl", "x", "z")


def dft_columns():
    col = np.arange(COLS)
    channel = CH0 + col // 2
    m = (np.arange(NFFT)[:, None] * channel[None, :]) % NFFT
    angle = m * (2.0 * math.pi / NFFT)
    table = np.where((col % 2 == 0)[None, :], np.cos(angle), -np.sin(angle)) / math.sqrt(NFFT)
    return jnp.asarray(table.astype(np.float32)).astype(jnp.bfloat16)


def pair_sum(terms):
    terms = list(terms)
    while len(terms) > 1:
        terms = [
            terms[i] + terms[i + 1] if i + 1 < len(terms) else terms[i]
            for i in range(0, len(terms), 2)
        ]
    return terms[0]


def accumulate(first_in, count_in, first_out, x_ref, w_ref, d_ref, filt_ref, acc_ref):
    weights = [
        jnp.broadcast_to(w_ref[p : p + 1, :], (8, NT)).astype(jnp.bfloat16) for p in range(TAPS)
    ]

    def group(s, carry):
        held = {}
        rows = []
        for g in range(first_out, first_out + HALF):
            frames = [f for f in range(g - TAPS + 1, g + 1) if first_in <= f < first_in + count_in]
            for f in frames:
                if f not in held:
                    held[f] = x_ref[s, f - first_in]
            if frames:
                rows.append(pair_sum(held[f] * weights[f - g + TAPS - 1] for f in frames))
            else:
                rows.append(jnp.zeros((8, NT), jnp.bfloat16))
        for k in range(HALF):
            filt_ref[k, s] = rows[k]
        return carry

    lax.fori_loop(0, SIG // 8, group, 0, unroll=8)

    def frames_part(k, carry):
        part = jnp.dot(
            filt_ref[pl.ds(k * 4, 4)].reshape(4 * SIG, NT),
            d_ref[...],
            preferred_element_type=jnp.float32,
        )
        acc_ref[pl.ds(k * 4, 4)] += part.reshape(4, SIG, COLS)
        return carry

    lax.fori_loop(0, HALF // 4, frames_part, 0, unroll=True)


def tail_kernel(first_in, count_in, x_ref, w_ref, d_ref, o_ref, filt_ref, acc_ref):
    @pl.when(pl.program_id(0) == 0)
    def _():
        acc_ref[...] = jnp.zeros_like(acc_ref)

    accumulate(first_in, count_in, FRAMES, x_ref, w_ref, d_ref, filt_ref, acc_ref)

    @pl.when(pl.program_id(0) == pl.num_programs(0) - 1)
    def _():
        o_ref[...] = acc_ref[...].astype(o_ref.dtype)


def emit(acc_ref, turn_ref, o_ref):
    for k in range(HALF // 2):
        block = acc_ref[2 * k : 2 * k + 2].reshape(2 * SIG, COLS)
        turn_ref[pl.ds(k, COLS, stride=HALF // 2), :] = block.T
    value = turn_ref[...].astype(o_ref.dtype).reshape(GROUPS, 64, 128)
    o_ref[0, :, 0] = value
    o_ref[1, :, 0] = value


def late_kernel(x_ref, w_ref, d_ref, o_ref, filt_ref, acc_ref, turn_ref):
    @pl.when(pl.program_id(0) == 0)
    def _():
        acc_ref[...] = jnp.zeros_like(acc_ref)

    accumulate(0, FRAMES, HALF, x_ref, w_ref, d_ref, filt_ref, acc_ref)

    @pl.when(pl.program_id(0) == pl.num_programs(0) - 1)
    def _():
        emit(acc_ref, turn_ref, o_ref)


def early_kernel(x_ref, w_ref, d_ref, halo_ref, late_ref, o_ref, filt_ref, acc_ref, turn_ref):
    del late_ref

    @pl.when(pl.program_id(0) == 0)
    def _():
        acc_ref[...] = halo_ref[...].astype(jnp.float32)

    accumulate(0, HALF, 0, x_ref, w_ref, d_ref, filt_ref, acc_ref)

    @pl.when(pl.program_id(0) == pl.num_programs(0) - 1)
    def _():
        emit(acc_ref, turn_ref, o_ref)


def slab_specs(count_in, block):
    return [
        pl.BlockSpec((SIG // 8, count_in, 8, NT), lambda i: (0, block, 0, i)),
        pl.BlockSpec((TAPS, NT), lambda i: (0, i)),
        pl.BlockSpec((NT, COLS), lambda i: (i, 0)),
    ]


def params():
    return pltpu.CompilerParams(vmem_limit_bytes=48 * MIB)


def filt_shape():
    return pltpu.VMEM((HALF, SIG // 8, 8, NT), jnp.bfloat16)


def acc_shape():
    return pltpu.VMEM((HALF, SIG, COLS), jnp.float32)


def turn_shape():
    return pltpu.VMEM((COLS * HALF // 2, 128), jnp.float32)


def spectra_tail(x4, taps, table):
    return pl.pallas_call(
        functools.partial(tail_kernel, HALF, HALF),
        grid=(NFFT // NT,),
        in_specs=slab_specs(HALF, 1),
        out_specs=pl.BlockSpec((HALF, SIG, COLS), lambda i: (0, 0, 0)),
        out_shape=jax.ShapeDtypeStruct((HALF, SIG, COLS), jnp.bfloat16),
        scratch_shapes=[filt_shape(), acc_shape()],
        compiler_params=params(),
        cost_estimate=pl.CostEstimate(flops=600_000_000, bytes_accessed=6 * MIB, transcendentals=0),
        name="spectra_tail",
    )(x4, taps, table)


VOLT_SHAPE = (2, GROUPS, 2, 64, 128)


def spectra_late(x4, taps, table):
    return pl.pallas_call(
        late_kernel,
        grid=(NFFT // NT,),
        in_specs=slab_specs(FRAMES, 0),
        out_specs=pl.BlockSpec((2, GROUPS, 1, 64, 128), lambda i: (0, 0, 1, 0, 0)),
        out_shape=jax.ShapeDtypeStruct(VOLT_SHAPE, jnp.bfloat16),
        scratch_shapes=[filt_shape(), acc_shape(), turn_shape()],
        compiler_params=params(),
        cost_estimate=pl.CostEstimate(flops=2_000_000_000, bytes_accessed=11 * MIB, transcendentals=0),
        name="spectra_late",
    )(x4, taps, table)


def spectra_early(x4, taps, table, halo, late):
    return pl.pallas_call(
        early_kernel,
        grid=(NFFT // NT,),
        in_specs=slab_specs(HALF, 0)
        + [
            pl.BlockSpec((HALF, SIG, COLS), lambda i: (0, 0, 0)),
            pl.BlockSpec(memory_space=pl.ANY),
        ],
        out_specs=pl.BlockSpec((2, GROUPS, 1, 64, 128), lambda i: (0, 0, 0, 0, 0)),
        out_shape=jax.ShapeDtypeStruct(VOLT_SHAPE, jnp.bfloat16),
        scratch_shapes=[filt_shape(), acc_shape(), turn_shape()],
        input_output_aliases={4: 0},
        compiler_params=params(),
        cost_estimate=pl.CostEstimate(flops=600_000_000, bytes_accessed=7 * MIB, transcendentals=0),
        name="spectra_early",
    )(x4, taps, table, halo, late)


def correlate_kernel(scale, tm_ref, own_ref, other_ref, o_ref, all_ref, left_ref):
    pairs = GROUPS // 2

    @pl.when(pl.program_id(1) == 0)
    def _():
        def gather(q, carry):
            at = pl.ds(pl.multiple_of(q * 128, 128), 128)
            for c, ref in enumerate((own_ref, other_ref)):
                for y in range(2):
                    for h in range(2):
                        t0 = ref[y * GROUPS + 2 * q, h, 0]
                        t1 = ref[y * GROUPS + 2 * q + 1, h, 0]
                        even = jnp.concatenate([t0[:, :SIG], t1[:, :SIG]], axis=1)
                        odd = jnp.concatenate([t0[:, SIG:], t1[:, SIG:]], axis=1)
                        k = ((c * 2 + y) * 2 + h) * 16
                        all_ref[k : k + 16, at] = jnp.concatenate([even[:8], odd[:8]], axis=0)
                        all_ref[128 + k : 144 + k, at] = jnp.concatenate(
                            [even[8:], odd[8:]], axis=0
                        )
            return carry

        lax.fori_loop(0, pairs, gather, 0, unroll=16)
        mine = pl.ds(pl.multiple_of(tm_ref[0] * 512, 512), 512)
        rows = all_ref[:, mine].T
        left_ref[:512] = rows
        left_ref[512:, :128] = rows[:, 128:]
        left_ref[512:, 128:] = -rows[:, :128]

    width = o_ref.shape[-1]
    first = pl.program_id(1) * width

    def columns(n, carry):
        from_ = pl.ds(pl.multiple_of(first + n * 256, 256), 256)
        to = pl.ds(pl.multiple_of(n * 256, 256), 256)
        both = jnp.dot(left_ref[...], all_ref[:, from_], preferred_element_type=jnp.float32)
        both = (both * scale).astype(jnp.bfloat16)
        o_ref[0, 0, :, to] = both[:512]
        o_ref[0, 1, :, to] = both[512:]
        return carry

    lax.fori_loop(0, width // 256, columns, 0, unroll=8)


def correlate(tm, own, other, signals, frames_all):
    shape = (2 * GROUPS, 2, CH_DEV, 16, 128)
    block = pl.BlockSpec((2 * GROUPS, 2, 1, 16, 128), lambda j, n, t: (0, 0, j, 0, 0))
    width = signals // 1
    return pl.pallas_call(
        functools.partial(correlate_kernel, 1.0 / frames_all),
        grid_spec=pltpu.PrefetchScalarGridSpec(
            num_scalar_prefetch=1,
            grid=(CH_DEV, signals // width),
            in_specs=[block, block],
            out_specs=pl.BlockSpec((1, 2, 512, width), lambda j, n, t: (j, 0, 0, n)),
            scratch_shapes=[
                pltpu.VMEM((256, signals), jnp.bfloat16),
                pltpu.VMEM((1024, 256), jnp.bfloat16),
            ],
        ),
        out_shape=jax.ShapeDtypeStruct((CH_DEV, 2, 512, signals), jnp.bfloat16),
        compiler_params=params(),
        cost_estimate=pl.CostEstimate(flops=4_300_000_000, bytes_accessed=20 * MIB, transcendentals=0),
        name="correlate",
    )(tm, own.reshape(shape), other.reshape(shape))


def per_device(samples, tap_weights):
    x4 = samples.reshape(SIG // 8, 8, FRAMES, NFFT).transpose(0, 2, 1, 3)
    table = dft_columns()
    tail = spectra_tail(x4, tap_weights, table)
    halo = lax.ppermute(tail, ("yh", "core"), [(0, 1), (1, 2), (2, 3)])
    late = spectra_late(x4, tap_weights, table)
    volts = spectra_early(x4, tap_weights, table, halo, late)
    volts = volts.reshape(2 * GROUPS, 128, 128)
    own = lax.all_to_all(volts, PEERS, split_axis=0, concat_axis=0, tiled=True)
    other = lax.ppermute(own, "core", [(0, 1), (1, 0)])
    tm = (lax.axis_index("yh") * 2 + lax.axis_index("core")).astype(jnp.int32).reshape(1)
    return correlate(tm, own, other, GROUPS * SIG, FRAMES * 4)


def solution(mesh):
    fine = Mesh(
        mesh.devices.reshape(2, 2, 2, 4, 4),
        ("yh", "core", "yl", "x", "z"),
    )
    return jax.shard_map(
        per_device,
        mesh=fine,
        in_specs=(P(("yl", "x", "z"), ("yh", "core")), P()),
        out_specs=P(("yl", "x", "z"), None, ("yh", "core"), None),
        check_vma=False,
    )
```

time: 319 us -> 80.2 us (0.25)
  local copies, waits for them, and re-layouts: 109 us -> 2.13 us
  waiting for transfers between devices: 85.5 us -> 3.92 us
  matrix products: 80.6 us -> 0 us
  blocking collectives: 0 us -> 35.3 us
  Pallas kernels: 0 us -> 28.4 us
  other arithmetic: 23.8 us -> 0 us
  starting transfers between devices: 17.9 us -> 9.93 us
    dot_general x3 -> x0, matrix products: 80.6 us -> none  [the longest x1 67 us: project(): lax.dot_general(dft_rows, flat_rows, (((1,), (1,)), ((), ())), precision=...]
    all_to_all x1 -> x0, waiting for transfers between devices: 51.6 us -> none  [per_device(): lax.all_to_all(outgoing, ('tm', 'chan'), split_axis=0, concat_axis=0, til...]
    all_to_all x0 -> x1, blocking collectives: none -> 35.3 us  [per_device(): own = lax.all_to_all(volts, PEERS, split_axis=0, concat_axis=0, tiled=True)]
    ppermute x1 -> x2, waiting for transfers between devices: 33.9 us -> 3.92 us  [the longest x1 3.92 us: per_device(): other = lax.ppermute(own, 'core', [(0, 1), (1, 0)])]
    pallas_call x0 -> x4, Pallas kernels: none -> 28.4 us  [the longest x1 10.3 us: correlate(): pl.pallas_call(functools.partial(correlate_kernel, 1.0 / frames_all), gri...]
    reshape x2 -> x0, local copies, waits for them, and re-layouts: 20.8 us -> none  [the longest x1 12.3 us: to_columns(): turned_block.reshape(chan_count, parts_count * time_count * frame_count,...]
    another operation x1 -> x0, local copies, waits for them, and re-layouts: 19.4 us -> none  [to_columns(): block.reshape(time_count, source_count, chan_count, parts_count, signal_c...]
    transpose x1 -> x0, local copies, waits for them, and re-layouts: 19 us -> none  [to_columns(): turned_block = jnp.transpose(split_block, (2, 3, 0, 5, 1, 4))]
  transfers between devices with their start and end apart: 2 -> 2, of which waited for: 2 -> 1; matrix products, arithmetic and copies ran while one was open for 3% -> 0% of each run, Pallas kernels for 0% -> 10%
where the time goes in v1:
time: 80.2 us; the launch traced here: 79.8 us
  blocking collectives  35.3 us (44%)
  Pallas kernels  28.4 us (35%)
  starting transfers between devices  9.93 us (12%)
  waiting for transfers between devices  3.92 us (5%)
  local copies, waits for them, and re-layouts  2.13 us (3%)
    all_to_all x1, blocking collectives, per_device(): own = lax.all_to_all(volts, PEERS, split_axis=0, concat_axis=0, tiled=True)  35.3 us
    pallas_call x1, Pallas kernels, correlate(): pl.pallas_call(functools.partial(correlate_kernel, 1.0 / frames_all), gri...  10.3 us
    pallas_call x1, Pallas kernels, spectra_late(): pl.pallas_call(late_kernel, grid=(NFFT // NT,), in_specs=slab_specs(FRAME...  7.73 us
    ppermute x1, starting transfers between devices, per_device(): halo = lax.ppermute(tail, ('yh', 'core'), [(0, 1), (1, 2), (2, 3)])  6.21 us
    pallas_call x1, Pallas kernels, spectra_early(): pl.pallas_call(early_kernel, grid=(NFFT // NT,), in_specs=slab_specs(HALF...  5.51 us
    pallas_call x1, Pallas kernels, spectra_tail(): pl.pallas_call(functools.partial(tail_kernel, HALF, HALF), grid=(NFFT //...  4.87 us
    ppermute x1, waiting for transfers between devices, per_device(): other = lax.ppermute(own, 'core', [(0, 1), (1, 0)])  3.92 us
    ppermute x1, starting transfers between devices, per_device(): other = lax.ppermute(own, 'core', [(0, 1), (1, 0)])  3.72 us
  transfers between devices with their start and end apart: 2, of which 1 were waited for; matrix products, arithmetic and copies ran while one was open for 0% of the time, Pallas kernels for 10%

profile of v1, /device:TPU:1, one launch (start us, length us, event | category | flops | bytes accessed | tf_op | source)
XLA Modules:
  0.0 79.8 jit_solution(1069936253339300889)
XLA Ops:
  0.0 0.0 copy-start
  0.0 1.2 %copy-done = bf16[2048,256]{1,0:T(8,128)(2,1)S(1)} copy-done((bf16[2048,256]{1,0:T(8,128)(2,1)S(1)}, bf16[2048,256]{1,0:T(8,128)(2,1)}, u32[]{:S(2)}) %copy-start) | copy-done | bytes 1048600
  1.2 0.0 copy-start.1
  1.2 0.9 %copy-done.1 = f32[16,2048]{1,0:T(8,128)S(1)} copy-done((f32[16,2048]{1,0:T(8,128)S(1)}, f32[16,2048]{1,0:T(8,128)}, u32[]{:S(2)}) %copy-start.1) | copy-done | bytes 131096
  2.1 4.9 %spectra_tail.1 = bf16[16,64,256]{2,1,0:T(8,128)(2,1)S(1)} custom-call(bf16[8,32,8,2048]{3,2,1,0:T(8,128)(2,1)} %bitcast.9, f32[16,2048]{1,0:T(8,128)S(1)} %copy-done.1, bf16[2048,256]{1,0:T(8,128)(2,1)S(1)} %copy-done), custom_call_target="tpu_custom_call" | custom-call | flops 600000000 | bytes 6291456 | tf_op jit(solution)/shard_map/spectra_tail/pallas_call | solution.py:153
  7.0 6.2 %collective-permute-start = (bf16[16,64,256]{2,1,0:T(8,128)(2,1)S(1)}, bf16[16,64,256]{2,1,0:T(8,128)(2,1)S(1)}, u32[]{:S(2)}, u32[]{:S(2)}) collective-permute-start(bf16[16,64,256]{2,1,0:T(8,128)(2,1)S(1)} %spectra_tail.1), channel_id=1, source_target_pairs={{0,32},{32,64},{64,96},{1,33},{33,65},{65,97},{2,34},{34,66},{66,9... | collective-permute-start | bytes 1572872 | tf_op jit(solution)/shard_map/ppermute | solution.py:272
  13.2 7.7 %spectra_late.1.late_ref = bf16[2,32,2,64,128]{4,3,2,1,0:T(8,128)(2,1)S(1)} custom-call(bf16[8,32,8,2048]{3,2,1,0:T(8,128)(2,1)} %bitcast.10, f32[16,2048]{1,0:T(8,128)S(1)} %copy-done.1, bf16[2048,256]{1,0:T(8,128)(2,1)S(1)} %copy-done), custom_call_target="tpu_custom_call" | custom-call | flops 2000000000 | bytes 11534336 | tf_op jit(solution)/shard_map/spectra_late/pallas_call | solution.py:170
  21.0 0.0 collective-permute-done.halo_ref
  21.0 5.5 %spectra_early.1 = bf16[2,32,2,64,128]{4,3,2,1,0:T(8,128)(2,1)S(1)} custom-call(bf16[8,32,8,2048]{3,2,1,0:T(8,128)(2,1)} %bitcast.11, f32[16,2048]{1,0:T(8,128)S(1)} %copy-done.1, bf16[2048,256]{1,0:T(8,128)(2,1)S(1)} %copy-done, bf16[16,64,256]{2,1,0:T(8,128)(2,1)S(1)} %collective-permute-done.halo_ref, ...), custom_call_target="tpu_custom_call", output_to_operand_aliasing={{}: (4, {})} | custom-call | flops 600000000 | bytes 7340032 | tf_op jit(solution)/shard_map/spectra_early/pallas_call | solution.py:184
  26.5 35.3 %all_to_all.5 = bf16[64,128,128]{2,1,0:T(8,128)(2,1)S(1)} all-to-all(bf16[64,128,128]{2,1,0:T(8,128)(2,1)S(1)} %bitcast.7), channel_id=1, replica_groups=mesh['yh'=2,'core'=2,'yl'=2,'x'=4,'z'=4] {'yh','yl','x','z'}, dimensions={0} | all-to-all | bytes 4194304 | tf_op jit(solution)/shard_map/all_to_all | solution.py:276
  61.8 3.7 %collective-permute-start.1 = (bf16[64,128,128]{2,1,0:T(8,128)(2,1)S(1)}, bf16[64,128,128]{2,1,0:T(8,128)(2,1)}, u32[]{:S(2)}, u32[]{:S(2)}) collective-permute-start(bf16[64,128,128]{2,1,0:T(8,128)(2,1)S(1)} %all_to_all.5), channel_id=1, source_target_pairs={{0,32},{32,0},{1,33},{33,1},{2,34},{34,2},{3,35},{35,3},{4,36},{36... | collective-permute-start | bytes 6291464 | tf_op jit(solution)/shard_map/ppermute | solution.py:277
  65.5 3.9 %collective-permute-done.1 = bf16[64,128,128]{2,1,0:T(8,128)(2,1)} collective-permute-done((bf16[64,128,128]{2,1,0:T(8,128)(2,1)S(1)}, bf16[64,128,128]{2,1,0:T(8,128)(2,1)}, u32[]{:S(2)}, u32[]{:S(2)}) %collective-permute-start.1) | collective-permute-done | bytes 2097184 | tf_op jit(solution)/shard_map/ppermute | solution.py:277
  69.4 10.3 %correlate.1 = bf16[4,2,512,2048]{3,2,1,0:T(8,128)(2,1)} custom-call(s32[1]{0:T(128)} %bitcast.tm_ref, bf16[64,2,4,16,128]{4,3,2,1,0:T(8,128)(2,1)S(1)} %bitcast.8, bf16[64,2,4,16,128]{4,3,2,1,0:T(8,128)(2,1)} %bitcast.6.other_ref), custom_call_target="tpu_custom_call" | custom-call | flops 4300000256 | bytes 20971520 | tf_op jit(solution)/shard_map/correlate/pallas_call | solution.py:249
Async XLA Ops:
  0.0 1.2 %copy-start = (bf16[2048,256]{1,0:T(8,128)(2,1)S(1)}, bf16[2048,256]{1,0:T(8,128)(2,1)}, u32[]{:S(2)}) copy-start(bf16[2048,256]{1,0:T(8,128)(2,1)} %constant.15.d_ref) | copy-start | bytes 3145732
  1.2 0.9 %copy-start.1 = (f32[16,2048]{1,0:T(8,128)S(1)}, f32[16,2048]{1,0:T(8,128)}, u32[]{:S(2)}) copy-start(f32[16,2048]{1,0:T(8,128)} %w_ref.5) | copy-start | bytes 393220
  7.0 14.0 %collective-permute-start = (bf16[16,64,256]{2,1,0:T(8,128)(2,1)S(1)}, bf16[16,64,256]{2,1,0:T(8,128)(2,1)S(1)}, u32[]{:S(2)}, u32[]{:S(2)}) collective-permute-start(bf16[16,64,256]{2,1,0:T(8,128)(2,1)S(1)} %spectra_tail.1), channel_id=1, source_target_pairs={{0,32},{32,64},{64,96},{1,33},{33,65},{65,97},{2,34},{34,66},{66,9... | collective-permute-start | bytes 1572872 | tf_op jit(solution)/shard_map/ppermute | solution.py:272
  61.8 7.6 %collective-permute-start.1 = (bf16[64,128,128]{2,1,0:T(8,128)(2,1)S(1)}, bf16[64,128,128]{2,1,0:T(8,128)(2,1)}, u32[]{:S(2)}, u32[]{:S(2)}) collective-permute-start(bf16[64,128,128]{2,1,0:T(8,128)(2,1)S(1)} %all_to_all.5), channel_id=1, source_target_pairs={{0,32},{32,0},{1,33},{33,1},{2,34},{34,2},{3,35},{35,3},{4,36},{36... | collective-permute-start | bytes 6291464 | tf_op jit(solution)/shard_map/ppermute | solution.py:277

commit v2 on v1

v2 whole, which is shorter than its diff:
```python
import functools
import math

import jax
import jax.numpy as jnp
import numpy as np
from jax import lax
from jax.experimental import pallas as pl
from jax.experimental.pallas import tpu as pltpu
from jax.sharding import Mesh
from jax.sharding import PartitionSpec as P

NFFT = 2048
TAPS = 16
CH0 = 256
CH_DEV = 4
GROUPS = 32
COLS = GROUPS * CH_DEV * 2
SIG = 64
FRAMES = 32
HALF = 16
NT = 512
LANES = 256
SEND = 4
MIB = 2**20
TAIL_MIB = 48
PEERS = ("yh", "yl", "x", "z")


def dft_columns():
    col = np.arange(COLS)
    channel = CH0 + col // 2
    m = (np.arange(NFFT)[:, None] * channel[None, :]) % NFFT
    angle = m * (2.0 * math.pi / NFFT)
    table = np.where((col % 2 == 0)[None, :], np.cos(angle), -np.sin(angle)) / math.sqrt(NFFT)
    return jnp.asarray(table.astype(np.float32)).astype(jnp.bfloat16)


def pair_sum(terms):
    terms = list(terms)
    while len(terms) > 1:
        terms = [
            terms[i] + terms[i + 1] if i + 1 < len(terms) else terms[i]
            for i in range(0, len(terms), 2)
        ]
    return terms[0]


def accumulate(first_in, count_in, first_out, count_out, x_ref, w_ref, d_ref, filt_ref, acc_ref):
    for n in range(0, NT, LANES):
        lanes = slice(n, n + LANES)
        weights = [
            jnp.broadcast_to(w_ref[p : p + 1, lanes], (8, LANES)).astype(jnp.bfloat16)
            for p in range(TAPS)
        ]
        for s in range(SIG // 8):
            held = {}
            for g in range(first_out, first_out + count_out):
                frames = [
                    f for f in range(g - TAPS + 1, g + 1) if first_in <= f < first_in + count_in
                ]
                held = {
                    f: held[f] if f in held else x_ref[s, f - first_in, :, lanes] for f in frames
                }
                if frames:
                    row = pair_sum(held[f] * weights[f - g + TAPS - 1] for f in frames)
                else:
                    row = jnp.zeros((8, LANES), jnp.bfloat16)
                filt_ref[g - first_out, s, :, lanes] = row
    for k in range(0, count_out, 4):
        part = jnp.dot(
            filt_ref[k : k + 4].reshape(4 * SIG, NT),
            d_ref[...],
            preferred_element_type=jnp.float32,
        )
        acc_ref[k : k + 4] += part.reshape(4, SIG, COLS)


def tail_kernel(first_in, count_in, x_ref, w_ref, d_ref, o_ref, filt_ref, acc_ref):
    @pl.when(pl.program_id(0) == 0)
    def _():
        acc_ref[...] = jnp.zeros_like(acc_ref)

    accumulate(first_in, count_in, FRAMES, HALF, x_ref, w_ref, d_ref, filt_ref, acc_ref)

    @pl.when(pl.program_id(0) == pl.num_programs(0) - 1)
    def _():
        o_ref[...] = acc_ref[...].astype(o_ref.dtype)


def emit(acc, turn_ref, o_ref):
    for k in range(HALF // 2):
        block = acc(2 * k).reshape(2 * SIG, COLS)
        turn_ref[pl.ds(k, COLS, stride=HALF // 2), :] = block.T
    value = turn_ref[...].astype(o_ref.dtype).reshape(GROUPS, 64, 128)
    o_ref[0, :, 0] = value
    o_ref[1, :, 0] = value


def main_kernel(x_ref, w_ref, d_ref, o_ref, early_ref, filt_ref, acc_ref, turn_ref):
    @pl.when(pl.program_id(0) == 0)
    def _():
        acc_ref[...] = jnp.zeros_like(acc_ref)

    accumulate(0, FRAMES, 0, FRAMES, x_ref, w_ref, d_ref, filt_ref, acc_ref)

    @pl.when(pl.program_id(0) == pl.num_programs(0) - 1)
    def _():
        early_ref[...] = acc_ref[:HALF]
        emit(lambda k: acc_ref[HALF + k : HALF + k + 2], turn_ref, o_ref)


def join_kernel(early_ref, halo_ref, late_ref, o_ref, turn_ref):
    del late_ref
    emit(
        lambda k: early_ref[k : k + 2] + halo_ref[k : k + 2].astype(jnp.float32), turn_ref, o_ref
    )


def slab_specs(count_in, block):
    return [
        pl.BlockSpec((SIG // 8, count_in, 8, NT), lambda i: (0, block, 0, i)),
        pl.BlockSpec((TAPS, NT), lambda i: (0, i)),
        pl.BlockSpec((NT, COLS), lambda i: (i, 0)),
    ]


def params(mib=48):
    return pltpu.CompilerParams(vmem_limit_bytes=mib * MIB)


def filt_shape(frames):
    return pltpu.VMEM((frames, SIG // 8, 8, NT), jnp.bfloat16)


def acc_shape(frames):
    return pltpu.VMEM((frames, SIG, COLS), jnp.float32)


def turn_shape():
    return pltpu.VMEM((COLS * HALF // 2, 128), jnp.float32)


def spectra_tail(x4, taps, table):
    return pl.pallas_call(
        functools.partial(tail_kernel, HALF, HALF),
        grid=(NFFT // NT,),
        in_specs=slab_specs(HALF, 1),
        out_specs=pl.BlockSpec((HALF, SIG, COLS), lambda i: (0, 0, 0)),
        out_shape=jax.ShapeDtypeStruct((HALF, SIG, COLS), jnp.bfloat16),
        scratch_shapes=[filt_shape(HALF), acc_shape(HALF)],
        compiler_params=params(TAIL_MIB),
        cost_estimate=pl.CostEstimate(flops=600_000_000, bytes_accessed=6 * MIB, transcendentals=0),
        name="spectra_tail",
    )(x4, taps, table)


VOLT_SHAPE = (2, GROUPS, 2, 64, 128)


def spectra_main(x4, taps, table):
    return pl.pallas_call(
        main_kernel,
        grid=(NFFT // NT,),
        in_specs=slab_specs(FRAMES, 0),
        out_specs=[
            pl.BlockSpec((2, GROUPS, 1, 64, 128), lambda i: (0, 0, 1, 0, 0)),
            pl.BlockSpec((HALF, SIG, COLS), lambda i: (0, 0, 0)),
        ],
        out_shape=[
            jax.ShapeDtypeStruct(VOLT_SHAPE, jnp.bfloat16),
            jax.ShapeDtypeStruct((HALF, SIG, COLS), jnp.float32),
        ],
        scratch_shapes=[filt_shape(FRAMES), acc_shape(FRAMES), turn_shape()],
        compiler_params=params(),
        cost_estimate=pl.CostEstimate(flops=2_600_000_000, bytes_accessed=12 * MIB, transcendentals=0),
        name="spectra_main",
    )(x4, taps, table)


def spectra_join(early, halo, late):
    return pl.pallas_call(
        join_kernel,
        grid=(1,),
        in_specs=[
            pl.BlockSpec((HALF, SIG, COLS), lambda i: (0, 0, 0)),
            pl.BlockSpec((HALF, SIG, COLS), lambda i: (0, 0, 0)),
            pl.BlockSpec(memory_space=pl.ANY),
        ],
        out_specs=pl.BlockSpec((2, GROUPS, 1, 64, 128), lambda i: (0, 0, 0, 0, 0)),
        out_shape=jax.ShapeDtypeStruct(VOLT_SHAPE, jnp.bfloat16),
        scratch_shapes=[turn_shape()],
        input_output_aliases={2: 0},
        compiler_params=params(),
        cost_estimate=pl.CostEstimate(flops=1_000_000, bytes_accessed=3 * MIB, transcendentals=0),
        name="spectra_join",
    )(early, halo, late)


def gather(j, own_ref, other_ref, all_ref, q):
    at = slice(q * 2 * SIG, (q + 1) * 2 * SIG)
    for c, ref in enumerate((own_ref, other_ref)):
        for y in range(2):
            for h in range(2):
                t0 = ref[y * GROUPS + 2 * q, h, j]
                t1 = ref[y * GROUPS + 2 * q + 1, h, j]
                even = jnp.concatenate([t0[:, :SIG], t1[:, :SIG]], axis=1)
                odd = jnp.concatenate([t0[:, SIG:], t1[:, SIG:]], axis=1)
                k = ((c * 2 + y) * 2 + h) * 16
                all_ref[k : k + 16, at] = jnp.concatenate([even[:8], odd[:8]], axis=0)
                all_ref[128 + k : 144 + k, at] = jnp.concatenate([even[8:], odd[8:]], axis=0)


def turn(tm_ref, all_ref, left_ref):
    mine = pl.ds(pl.multiple_of(tm_ref[0] * 512, 512), 512)
    rows = all_ref[:, mine].T
    left_ref[:512] = rows
    left_ref[512:, :128] = rows[:, 128:]
    left_ref[512:, 128:] = -rows[:, :128]


def correlate_kernel(scale, tm_ref, own_ref, other_ref, o_ref, *scratch):
    alls, lefts, stages, sem = scratch[:2], scratch[2:4], scratch[4:6], scratch[6]
    tiles = o_ref.shape[-1] // 256
    pairs = GROUPS // 2 // tiles
    flying = {}
    for q in range(GROUPS // 2):
        gather(0, own_ref, other_ref, alls[0], q)
    turn(tm_ref, alls[0], lefts[0])
    for j in range(CH_DEV):
        slot, other_slot = j % 2, (j + 1) % 2
        stage = stages[slot]
        for n in range(tiles):
            cols = slice(n * 256, n * 256 + 256)
            piece = n // SEND
            if n % SEND == 0 and (slot, piece) in flying:
                flying.pop((slot, piece)).wait()
            both = jnp.dot(
                lefts[slot][...], alls[slot][:, cols], preferred_element_type=jnp.float32
            )
            both = (both * scale).astype(jnp.bfloat16)
            stage[0, :, cols] = both[:512]
            stage[1, :, cols] = both[512:]
            if j + 1 < CH_DEV:
                for q in range(n * pairs, (n + 1) * pairs):
                    gather(j + 1, own_ref, other_ref, alls[other_slot], q)
            if n % SEND == SEND - 1:
                wide = slice(piece * SEND * 256, (piece + 1) * SEND * 256)
                copy = pltpu.make_async_copy(
                    stage.at[:, :, wide], o_ref.at[j, :, :, wide], sem.at[slot, piece]
                )
                copy.start()
                flying[slot, piece] = copy
        if j + 1 < CH_DEV:
            turn(tm_ref, alls[other_slot], lefts[other_slot])
    for copy in flying.values():
        copy.wait()


def correlate(tm, own, other, signals, frames_all):
    shape = (2 * GROUPS, 2, CH_DEV, 16, 128)
    return pl.pallas_call(
        functools.partial(correlate_kernel, 1.0 / frames_all),
        in_specs=[
            pl.BlockSpec(memory_space=pltpu.SMEM),
            pl.BlockSpec(memory_space=pltpu.VMEM),
            pl.BlockSpec(memory_space=pltpu.VMEM),
        ],
        out_specs=pl.BlockSpec(memory_space=pl.ANY),
        out_shape=jax.ShapeDtypeStruct((CH_DEV, 2, 512, signals), jnp.bfloat16),
        scratch_shapes=[pltpu.VMEM((256, signals), jnp.bfloat16)] * 2
        + [pltpu.VMEM((1024, 256), jnp.bfloat16)] * 2
        + [pltpu.VMEM((2, 512, signals), jnp.bfloat16)] * 2
        + [pltpu.SemaphoreType.DMA((2, signals // 256 // SEND))],
        compiler_params=params(),
        cost_estimate=pl.CostEstimate(flops=4_300_000_000, bytes_accessed=20 * MIB, transcendentals=0),
        name="correlate",
    )(tm, own.reshape(shape), other.reshape(shape))


def per_device(samples, tap_weights):
    x4 = samples.reshape(SIG // 8, 8, FRAMES, NFFT).transpose(0, 2, 1, 3)
    table = dft_columns()
    tail = spectra_tail(x4, tap_weights, table)
    halo = lax.ppermute(tail, ("yh", "core"), [(0, 1), (1, 2), (2, 3)])
    late, early = spectra_main(x4, tap_weights, table)
    volts = spectra_join(early, halo, late)
    volts = volts.reshape(2 * GROUPS, 128, 128)
    own = lax.all_to_all(volts, PEERS, split_axis=0, concat_axis=0, tiled=True)
    other = lax.ppermute(own, "core", [(0, 1), (1, 0)])
    tm = (lax.axis_index("yh") * 2 + lax.axis_index("core")).astype(jnp.int32).reshape(1)
    return correlate(tm, own, other, GROUPS * SIG, FRAMES * 4)


def solution(mesh):
    fine = Mesh(
        mesh.devices.reshape(2, 2, 2, 4, 4),
        ("yh", "core", "yl", "x", "z"),
    )
    return jax.shard_map(
        per_device,
        mesh=fine,
        in_specs=(P(("yl", "x", "z"), ("yh", "core")), P()),
        out_specs=P(("yl", "x", "z"), None, ("yh", "core"), None),
        check_vma=False,
    )
```

time: 80.2 us -> 75.7 us (0.944)
  Pallas kernels: 28.4 us -> 24.5 us
  starting transfers between devices: 9.93 us -> 7.4 us
  blocking collectives: 35.3 us -> 37.5 us
    pallas_call x3, Pallas kernels: 23.6 us -> 19.6 us  [the longest x1 10.3 us: spectra_main(): pl.pallas_call(main_kernel, grid=(NFFT // NT,), in_specs=slab_specs(FRAME...]
    ppermute x1, starting transfers between devices: 3.72 us -> 1.18 us  [per_device(): other = lax.ppermute(own, 'core', [(0, 1), (1, 0)])]
    all_to_all x1, blocking collectives: 35.3 us -> 37.5 us  [per_device(): own = lax.all_to_all(volts, PEERS, split_axis=0, concat_axis=0, tiled=True)]
  transfers between devices with their start and end apart: 2 -> 2, of which waited for: 1 -> 1; matrix products, arithmetic and copies ran while one was open for 0% -> 0% of each run, Pallas kernels for 10% -> 14%
where the time goes in v2:
time: 75.7 us; the launch traced here: 75.4 us
  blocking collectives  37.5 us (50%)
  Pallas kernels  24.5 us (32%)
  starting transfers between devices  7.4 us (10%)
  waiting for transfers between devices  3.92 us (5%)
  local copies, waits for them, and re-layouts  2.13 us (3%)
    all_to_all x1, blocking collectives, per_device(): own = lax.all_to_all(volts, PEERS, split_axis=0, concat_axis=0, tiled=True)  37.5 us
    pallas_call x1, Pallas kernels, spectra_main(): pl.pallas_call(main_kernel, grid=(NFFT // NT,), in_specs=slab_specs(FRAME...  10.3 us
    pallas_call x1, Pallas kernels, correlate(): pl.pallas_call(functools.partial(correlate_kernel, 1.0 / frames_all), in_...  8.74 us
    ppermute x1, starting transfers between devices, per_device(): halo = lax.ppermute(tail, ('yh', 'core'), [(0, 1), (1, 2), (2, 3)])  6.21 us
    pallas_call x1, Pallas kernels, spectra_tail(): pl.pallas_call(functools.partial(tail_kernel, HALF, HALF), grid=(NFFT //...  4.86 us
    ppermute x1, waiting for transfers between devices, per_device(): other = lax.ppermute(own, 'core', [(0, 1), (1, 0)])  3.92 us
    unnamed x4, local copies, waits for them, and re-layouts  2.13 us
  transfers between devices with their start and end apart: 2, of which 1 were waited for; matrix products, arithmetic and copies ran while one was open for 0% of the time, Pallas kernels for 14%

profile of v2, /device:TPU:1, one launch (start us, length us, event | category | flops | bytes accessed | tf_op | source)
XLA Modules:
  0.0 75.4 jit_solution(10257878193670182076)
XLA Ops:
  0.0 0.0 copy-start
  0.0 1.2 %copy-done = bf16[2048,256]{1,0:T(8,128)(2,1)S(1)} copy-done((bf16[2048,256]{1,0:T(8,128)(2,1)S(1)}, bf16[2048,256]{1,0:T(8,128)(2,1)}, u32[]{:S(2)}) %copy-start) | copy-done | bytes 1048600
  1.2 0.0 copy-start.1
  1.2 0.9 %copy-done.1 = f32[16,2048]{1,0:T(8,128)S(1)} copy-done((f32[16,2048]{1,0:T(8,128)S(1)}, f32[16,2048]{1,0:T(8,128)}, u32[]{:S(2)}) %copy-start.1) | copy-done | bytes 131096
  2.1 4.9 %spectra_tail.1 = bf16[16,64,256]{2,1,0:T(8,128)(2,1)S(1)} custom-call(bf16[8,32,8,2048]{3,2,1,0:T(8,128)(2,1)} %bitcast.9, f32[16,2048]{1,0:T(8,128)S(1)} %copy-done.1, bf16[2048,256]{1,0:T(8,128)(2,1)S(1)} %copy-done), custom_call_target="tpu_custom_call" | custom-call | flops 600000000 | bytes 6291456 | tf_op jit(solution)/shard_map/spectra_tail/pallas_call | solution.py:145
  7.0 6.2 %collective-permute-start = (bf16[16,64,256]{2,1,0:T(8,128)(2,1)S(1)}, bf16[16,64,256]{2,1,0:T(8,128)(2,1)S(1)}, u32[]{:S(2)}, u32[]{:S(2)}) collective-permute-start(bf16[16,64,256]{2,1,0:T(8,128)(2,1)S(1)} %spectra_tail.1), channel_id=1, source_target_pairs={{0,32},{32,64},{64,96},{1,33},{33,65},{65,97},{2,34},{34,66},{66,9... | collective-permute-start | bytes 1572872 | tf_op jit(solution)/shard_map/ppermute | solution.py:285
  13.2 10.3 %spectra_main.1 = (bf16[2,32,2,64,128]{4,3,2,1,0:T(8,128)(2,1)S(1)}, f32[16,64,256]{2,1,0:T(8,128)S(1)}) custom-call(bf16[8,32,8,2048]{3,2,1,0:T(8,128)(2,1)} %bitcast.10, f32[16,2048]{1,0:T(8,128)S(1)} %copy-done.1, bf16[2048,256]{1,0:T(8,128)(2,1)S(1)} %copy-done), custom_call_target="tpu_custom_call" | custom-call | flops 2600000000 | bytes 12582912 | tf_op jit(solution)/shard_map/spectra_main/pallas_call | solution.py:162
  23.5 0.0 collective-permute-done.halo_ref
  23.6 0.5 spectra_join.1
  24.1 37.5 %all_to_all.5 = bf16[64,128,128]{2,1,0:T(8,128)(2,1)S(1)} all-to-all(bf16[64,128,128]{2,1,0:T(8,128)(2,1)S(1)} %bitcast.8), channel_id=1, replica_groups=mesh['yh'=2,'core'=2,'yl'=2,'x'=4,'z'=4] {'yh','yl','x','z'}, dimensions={0} | all-to-all | bytes 4194304 | tf_op jit(solution)/shard_map/all_to_all | solution.py:289
  61.6 1.2 %collective-permute-start.1 = (bf16[64,128,128]{2,1,0:T(8,128)(2,1)S(1)}, bf16[64,128,128]{2,1,0:T(8,128)(2,1)}, u32[]{:S(2)}, u32[]{:S(2)}) collective-permute-start(bf16[64,128,128]{2,1,0:T(8,128)(2,1)S(1)} %all_to_all.5), channel_id=1, source_target_pairs={{0,32},{32,0},{1,33},{33,1},{2,34},{34,2},{3,35},{35,3},{4,36},{36... | collective-permute-start | bytes 6291464 | tf_op jit(solution)/shard_map/ppermute | solution.py:290
  62.8 3.9 %collective-permute-done.1 = bf16[64,128,128]{2,1,0:T(8,128)(2,1)} collective-permute-done((bf16[64,128,128]{2,1,0:T(8,128)(2,1)S(1)}, bf16[64,128,128]{2,1,0:T(8,128)(2,1)}, u32[]{:S(2)}, u32[]{:S(2)}) %collective-permute-start.1) | collective-permute-done | bytes 2097184 | tf_op jit(solution)/shard_map/ppermute | solution.py:290
  66.7 8.7 %correlate.1 = bf16[4,2,512,2048]{3,2,1,0:T(8,128)(2,1)} custom-call(s32[1]{0:T(128)} %bitcast.tm_ref, bf16[64,2,4,16,128]{4,3,2,1,0:T(8,128)(2,1)S(1)} %bitcast.7, bf16[64,2,4,16,128]{4,3,2,1,0:T(8,128)(2,1)} %bitcast.6.other_ref), custom_call_target="tpu_custom_call" | custom-call | flops 4300000256 | bytes 20971520 | tf_op jit(solution)/shard_map/correlate/pallas_call | solution.py:262
Async XLA Ops:
  0.0 1.2 %copy-start = (bf16[2048,256]{1,0:T(8,128)(2,1)S(1)}, bf16[2048,256]{1,0:T(8,128)(2,1)}, u32[]{:S(2)}) copy-start(bf16[2048,256]{1,0:T(8,128)(2,1)} %constant.15.d_ref) | copy-start | bytes 3145732
  1.2 0.9 %copy-start.1 = (f32[16,2048]{1,0:T(8,128)S(1)}, f32[16,2048]{1,0:T(8,128)}, u32[]{:S(2)}) copy-start(f32[16,2048]{1,0:T(8,128)} %w_ref.3) | copy-start | bytes 393220
  7.0 16.5 %collective-permute-start = (bf16[16,64,256]{2,1,0:T(8,128)(2,1)S(1)}, bf16[16,64,256]{2,1,0:T(8,128)(2,1)S(1)}, u32[]{:S(2)}, u32[]{:S(2)}) collective-permute-start(bf16[16,64,256]{2,1,0:T(8,128)(2,1)S(1)} %spectra_tail.1), channel_id=1, source_target_pairs={{0,32},{32,64},{64,96},{1,33},{33,65},{65,97},{2,34},{34,66},{66,9... | collective-permute-start | bytes 1572872 | tf_op jit(solution)/shard_map/ppermute | solution.py:285
  61.6 5.1 %collective-permute-start.1 = (bf16[64,128,128]{2,1,0:T(8,128)(2,1)S(1)}, bf16[64,128,128]{2,1,0:T(8,128)(2,1)}, u32[]{:S(2)}, u32[]{:S(2)}) collective-permute-start(bf16[64,128,128]{2,1,0:T(8,128)(2,1)S(1)} %all_to_all.5), channel_id=1, source_target_pairs={{0,32},{32,0},{1,33},{33,1},{2,34},{34,2},{3,35},{35,3},{4,36},{36... | collective-permute-start | bytes 6291464 | tf_op jit(solution)/shard_map/ppermute | solution.py:290

commit v3 on v2

v3 whole, which is shorter than its diff:
```python
import functools
import math

import jax
import jax.numpy as jnp
import numpy as np
from jax import lax
from jax.experimental import pallas as pl
from jax.experimental.pallas import tpu as pltpu
from jax.sharding import Mesh
from jax.sharding import PartitionSpec as P

NFFT = 2048
TAPS = 16
CH0 = 256
CH_DEV = 4
GROUPS = 32
COLS = GROUPS * CH_DEV * 2
SIG = 64
FRAMES = 32
HALF = 16
NT = 512
LANES = 256
SEND = 4
MIB = 2**20
TAIL_MIB = 24
MAIN_MIB = 24
JOIN_MIB = 24
CORR_MIB = 24
PEERS = ("yh", "yl", "x", "z")


def dft_columns():
    col = np.arange(COLS)
    channel = CH0 + col // 2
    m = (np.arange(NFFT)[:, None] * channel[None, :]) % NFFT
    angle = m * (2.0 * math.pi / NFFT)
    table = np.where((col % 2 == 0)[None, :], np.cos(angle), -np.sin(angle)) / math.sqrt(NFFT)
    return jnp.asarray(table.astype(np.float32)).astype(jnp.bfloat16)


def pair_sum(terms):
    terms = list(terms)
    while len(terms) > 1:
        terms = [
            terms[i] + terms[i + 1] if i + 1 < len(terms) else terms[i]
            for i in range(0, len(terms), 2)
        ]
    return terms[0]


def filtered(first_in, count_in, first_out, count_out, x, weights, filt_ref, lanes):
    for s in range(SIG // 8):
        held = {}
        for g in range(first_out, first_out + count_out):
            frames = [f for f in range(g - TAPS + 1, g + 1) if first_in <= f < first_in + count_in]
            held = {f: held[f] if f in held else x(s, f) for f in frames}
            if frames:
                row = pair_sum(held[f] * weights[f - g + TAPS - 1] for f in frames)
            else:
                row = jnp.zeros((8, LANES), jnp.bfloat16)
            filt_ref[g - first_out, s, :, lanes] = row


def accumulate(first_in, count_in, first_out, count_out, i, x_ref, w_ref, filt_ref):
    for n in range(0, NT, LANES):
        at = slice(i * NT + n, i * NT + n + LANES)
        weights = [
            jnp.broadcast_to(w_ref[p : p + 1, at], (8, LANES)).astype(jnp.bfloat16)
            for p in range(TAPS)
        ]
        filtered(
            first_in,
            count_in,
            first_out,
            count_out,
            lambda s, f: x_ref[s, f, :, at],
            weights,
            filt_ref,
            slice(n, n + LANES),
        )


def project(i, count_out, d_ref, filt_ref, acc_ref):
    table = d_ref[i * NT : i * NT + NT, :]
    for k in range(0, count_out, 4):
        part = jnp.dot(
            filt_ref[k : k + 4].reshape(4 * SIG, NT), table, preferred_element_type=jnp.float32
        )
        acc_ref[k : k + 4] += part.reshape(4, SIG, COLS)


def tail_kernel(
    x_ref, w_ref, d_ref, o_ref, x_out, w_out, d_out, filt_ref, acc_ref, sem, early_sem
):
    slabs = NFFT // NT

    def copy(first, i, sems):
        at = slice(i * NT, i * NT + NT)
        return pltpu.make_async_copy(
            x_ref.at[:, first : first + HALF, :, at],
            x_out.at[:, first : first + HALF, :, at],
            sems.at[i],
        )

    w_copy = pltpu.make_async_copy(w_ref, w_out, sem.at[slabs])
    d_copy = pltpu.make_async_copy(d_ref, d_out, sem.at[slabs + 1])
    w_copy.start()
    copy(HALF, 0, sem).start()
    copy(HALF, 1, sem).start()
    d_copy.start()
    acc_ref[...] = jnp.zeros_like(acc_ref)
    w_copy.wait()

    for i in range(slabs):
        copy(HALF, i, sem).wait()
        if i + 2 < slabs:
            copy(HALF, i + 2, sem).start()
        copy(0, i, early_sem).start()
        accumulate(HALF, HALF, FRAMES, HALF, i, x_out, w_out, filt_ref)
        if i == 0:
            d_copy.wait()
        project(i, HALF, d_out, filt_ref, acc_ref)
    o_ref[...] = acc_ref[...].astype(o_ref.dtype)
    for i in range(slabs):
        copy(0, i, early_sem).wait()


def emit(acc, turn_ref):
    for k in range(HALF // 2):
        block = acc(2 * k).reshape(2 * SIG, COLS)
        turn_ref[pl.ds(k, COLS, stride=HALF // 2), :] = block.T
    return turn_ref[...].astype(jnp.bfloat16).reshape(GROUPS, 64, 128)


def main_kernel(x_ref, w_ref, d_ref, o_ref, early_ref, filt_ref, acc_ref, turn_ref):
    @pl.when(pl.program_id(0) == 0)
    def _():
        acc_ref[...] = jnp.zeros_like(acc_ref)

    accumulate(0, FRAMES, 0, FRAMES, 0, x_ref, w_ref, filt_ref)
    project(0, FRAMES, d_ref, filt_ref, acc_ref)

    @pl.when(pl.program_id(0) == pl.num_programs(0) - 1)
    def _():
        early_ref[...] = acc_ref[:HALF]
        late = emit(lambda k: acc_ref[HALF + k : HALF + k + 2], turn_ref)
        o_ref[0, :, 0] = late
        o_ref[1, :, 0] = late


def join_kernel(early_ref, halo_ref, late_ref, o_ref, turn_ref):
    del late_ref

    def both(k):
        return early_ref[k : k + 2] + halo_ref[k : k + 2].astype(jnp.float32)

    early = emit(both, turn_ref)
    o_ref[0, :, 0] = early
    o_ref[1, :, 0] = early


def params(mib):
    return pltpu.CompilerParams(vmem_limit_bytes=mib * MIB)


def filt_shape(frames):
    return pltpu.VMEM((frames, SIG // 8, 8, NT), jnp.bfloat16)


def acc_shape(frames):
    return pltpu.VMEM((frames, SIG, COLS), jnp.float32)


def turn_shape():
    return pltpu.VMEM((COLS * HALF // 2, 128), jnp.float32)


VOLT_SHAPE = (2, GROUPS, 2, 64, 128)
VMEM = pl.BlockSpec(memory_space=pltpu.VMEM)


def spectra_tail(x4, taps, table):
    return pl.pallas_call(
        tail_kernel,
        in_specs=[pl.BlockSpec(memory_space=pltpu.HBM)] * 3,
        out_specs=[VMEM] * 4,
        out_shape=[
            jax.ShapeDtypeStruct((HALF, SIG, COLS), jnp.bfloat16),
            jax.ShapeDtypeStruct(x4.shape, x4.dtype),
            jax.ShapeDtypeStruct(taps.shape, taps.dtype),
            jax.ShapeDtypeStruct(table.shape, table.dtype),
        ],
        scratch_shapes=[
            filt_shape(HALF),
            acc_shape(HALF),
            pltpu.SemaphoreType.DMA((NFFT // NT + 2,)),
            pltpu.SemaphoreType.DMA((NFFT // NT,)),
        ],
        compiler_params=params(TAIL_MIB),
        cost_estimate=pl.CostEstimate(flops=600_000_000, bytes_accessed=9 * MIB, transcendentals=0),
        name="spectra_tail",
    )(x4, taps, table)


def spectra_main(x4, taps, table):
    return pl.pallas_call(
        main_kernel,
        grid=(NFFT // NT,),
        in_specs=[
            pl.BlockSpec((SIG // 8, FRAMES, 8, NT), lambda i: (0, 0, 0, i)),
            pl.BlockSpec((TAPS, NT), lambda i: (0, i)),
            pl.BlockSpec((NT, COLS), lambda i: (i, 0)),
        ],
        out_specs=[
            pl.BlockSpec((2, GROUPS, 1, 64, 128), lambda i: (0, 0, 1, 0, 0)),
            pl.BlockSpec((HALF, SIG, COLS), lambda i: (0, 0, 0)),
        ],
        out_shape=[
            jax.ShapeDtypeStruct(VOLT_SHAPE, jnp.bfloat16),
            jax.ShapeDtypeStruct((HALF, SIG, COLS), jnp.float32),
        ],
        scratch_shapes=[filt_shape(FRAMES), acc_shape(FRAMES), turn_shape()],
        compiler_params=params(MAIN_MIB),
        cost_estimate=pl.CostEstimate(flops=2_600_000_000, bytes_accessed=12 * MIB, transcendentals=0),
        name="spectra_main",
    )(x4, taps, table)


def spectra_join(early, halo, late):
    return pl.pallas_call(
        join_kernel,
        in_specs=[VMEM, VMEM, pl.BlockSpec(memory_space=pl.ANY)],
        out_specs=pl.BlockSpec(VOLT_SHAPE[:2] + (1, 64, 128), lambda i: (0, 0, 0, 0, 0)),
        grid=(1,),
        out_shape=jax.ShapeDtypeStruct(VOLT_SHAPE, jnp.bfloat16),
        scratch_shapes=[turn_shape()],
        input_output_aliases={2: 0},
        compiler_params=params(JOIN_MIB),
        cost_estimate=pl.CostEstimate(flops=1_000_000, bytes_accessed=3 * MIB, transcendentals=0),
        name="spectra_join",
    )(early, halo, late)


def gather(c, t, all_ref, q):
    at = slice(q * 2 * SIG, (q + 1) * 2 * SIG)
    for y in range(2):
        for h in range(2):
            t0 = t(y, 2 * q, h)
            t1 = t(y, 2 * q + 1, h)
            even = jnp.concatenate([t0[:, :SIG], t1[:, :SIG]], axis=1)
            odd = jnp.concatenate([t0[:, SIG:], t1[:, SIG:]], axis=1)
            k = ((c * 2 + y) * 2 + h) * 16
            all_ref[k : k + 16, at] = jnp.concatenate([even[:8], odd[:8]], axis=0)
            all_ref[128 + k : 144 + k, at] = jnp.concatenate([even[8:], odd[8:]], axis=0)


def turn(tm_ref, all_ref, left_ref):
    mine = pl.ds(pl.multiple_of(tm_ref[0] * 512, 512), 512)
    rows = all_ref[:, mine].T
    left_ref[:512] = rows
    left_ref[512:, :128] = rows[:, 128:]
    left_ref[512:, 128:] = -rows[:, :128]


def correlate_kernel(scale, tm_ref, own_ref, other_ref, o_ref, *scratch):
    alls, lefts, stages = scratch[:2], scratch[2:4], scratch[4:6]
    held_ref, sem, held_sem = scratch[6:]
    tiles = o_ref.shape[-1] // 256
    pairs = GROUPS // 2 // tiles
    flying = {}
    copies = [
        pltpu.make_async_copy(other_ref.at[:, :, j], held_ref.at[j], held_sem.at[j])
        for j in range(CH_DEV)
    ]
    for copy in copies:
        copy.start()

    def bring(j, c, q):
        if c == 0:
            gather(c, lambda y, g, h: own_ref[y * GROUPS + g, h, j], alls[j % 2], q)
        else:
            gather(c, lambda y, g, h: held_ref[j, y * GROUPS + g, h], alls[j % 2], q)

    for q in range(GROUPS // 2):
        bring(0, 0, q)
    copies[0].wait()
    for q in range(GROUPS // 2):
        bring(0, 1, q)
    turn(tm_ref, alls[0], lefts[0])
    for j in range(CH_DEV):
        slot, other_slot = j % 2, (j + 1) % 2
        stage = stages[slot]
        if j + 1 < CH_DEV:
            copies[j + 1].wait()
        for n in range(tiles):
            cols = slice(n * 256, n * 256 + 256)
            piece = n // SEND
            if n % SEND == 0 and (slot, piece) in flying:
                flying.pop((slot, piece)).wait()
            both = jnp.dot(
                lefts[slot][...], alls[slot][:, cols], preferred_element_type=jnp.float32
            )
            both = (both * scale).astype(jnp.bfloat16)
            stage[0, :, cols] = both[:512]
            stage[1, :, cols] = both[512:]
            if j + 1 < CH_DEV:
                for q in range(n * pairs, (n + 1) * pairs):
                    bring(j + 1, 0, q)
                    bring(j + 1, 1, q)
            if n % SEND == SEND - 1:
                wide = slice(piece * SEND * 256, (piece + 1) * SEND * 256)
                copy = pltpu.make_async_copy(
                    stage.at[:, :, wide], o_ref.at[j, :, :, wide], sem.at[slot, piece]
                )
                copy.start()
                flying[slot, piece] = copy
        if j + 1 < CH_DEV:
            turn(tm_ref, alls[other_slot], lefts[other_slot])
    for copy in flying.values():
        copy.wait()


def correlate(tm, own, other, signals, frames_all):
    shape = (2 * GROUPS, 2, CH_DEV, 16, 128)
    return pl.pallas_call(
        functools.partial(correlate_kernel, 1.0 / frames_all),
        in_specs=[
            pl.BlockSpec(memory_space=pltpu.SMEM),
            VMEM,
            pl.BlockSpec(memory_space=pl.ANY),
        ],
        out_specs=pl.BlockSpec(memory_space=pl.ANY),
        out_shape=jax.ShapeDtypeStruct((CH_DEV, 2, 512, signals), jnp.bfloat16),
        scratch_shapes=[pltpu.VMEM((256, signals), jnp.bfloat16)] * 2
        + [pltpu.VMEM((1024, 256), jnp.bfloat16)] * 2
        + [pltpu.VMEM((2, 512, signals), jnp.bfloat16)] * 2
        + [
            pltpu.VMEM((CH_DEV, 2 * GROUPS, 2, 16, 128), jnp.bfloat16),
            pltpu.SemaphoreType.DMA((2, signals // 256 // SEND)),
            pltpu.SemaphoreType.DMA((CH_DEV,)),
        ],
        compiler_params=params(CORR_MIB),
        cost_estimate=pl.CostEstimate(flops=4_300_000_000, bytes_accessed=20 * MIB, transcendentals=0),
        name="correlate",
    )(tm, own.reshape(shape), other.reshape(shape))


def front(samples, tap_weights, send):
    x4 = samples.reshape(SIG // 8, 8, FRAMES, NFFT).transpose(0, 2, 1, 3)
    operands = [pltpu.with_memory_space_constraint(v, pltpu.HBM) for v in (x4, tap_weights, dft_columns())]
    tail, *held = spectra_tail(*operands)
    halo = send(tail)
    late, early = spectra_main(*held)
    return spectra_join(early, halo, late).reshape(2 * GROUPS, 128, 128)


def per_device(samples, tap_weights):
    volts = front(
        samples,
        tap_weights,
        lambda v: lax.ppermute(v, ("yh", "core"), [(0, 1), (1, 2), (2, 3)]),
    )
    own = lax.all_to_all(volts, PEERS, split_axis=0, concat_axis=0, tiled=True)
    other = lax.ppermute(own, "core", [(0, 1), (1, 0)])
    tm = (lax.axis_index("yh") * 2 + lax.axis_index("core")).astype(jnp.int32).reshape(1)
    return correlate(tm, own, other, GROUPS * SIG, FRAMES * 4)


def solution(mesh):
    fine = Mesh(
        mesh.devices.reshape(2, 2, 2, 4, 4),
        ("yh", "core", "yl", "x", "z"),
    )
    return jax.shard_map(
        per_device,
        mesh=fine,
        in_specs=(P(("yl", "x", "z"), ("yh", "core")), P()),
        out_specs=P(("yl", "x", "z"), None, ("yh", "core"), None),
        check_vma=False,
    )
```

time: 75.7 us -> 72.8 us (0.962)
  local copies, waits for them, and re-layouts: 2.13 us -> 0 us
  starting transfers between devices: 7.4 us -> 8.7 us
  Pallas kernels: 24.5 us -> 23.3 us
  blocking collectives: 37.5 us -> 36.5 us
    unnamed x4 -> x0, local copies, waits for them, and re-layouts: 2.13 us -> none
    ppermute x1, starting transfers between devices: 1.18 us -> 2.49 us  [per_device(): other = lax.ppermute(own, 'core', [(0, 1), (1, 0)])]
    all_to_all x1, blocking collectives: 37.5 us -> 36.5 us  [per_device(): own = lax.all_to_all(volts, PEERS, split_axis=0, concat_axis=0, tiled=True)]
  transfers between devices with their start and end apart: 2 -> 2, of which waited for: 1 -> 1; matrix products, arithmetic and copies ran while one was open for 0% -> 0% of each run, Pallas kernels for 14% -> 13%
where the time goes in v3:
time: 72.8 us; the launch traced here: 72.6 us
  blocking collectives  36.5 us (50%)
  Pallas kernels  23.3 us (32%)
  starting transfers between devices  8.7 us (12%)
  waiting for transfers between devices  3.92 us (5%)
    all_to_all x1, blocking collectives, per_device(): own = lax.all_to_all(volts, PEERS, split_axis=0, concat_axis=0, tiled=True)  36.5 us
    pallas_call x1, Pallas kernels, spectra_main(): pl.pallas_call(main_kernel, grid=(NFFT // NT,), in_specs=[pl.BlockSpec((S...  9.35 us
    pallas_call x1, Pallas kernels, correlate(): pl.pallas_call(functools.partial(correlate_kernel, 1.0 / frames_all), in_...  8.28 us
    ppermute x1, starting transfers between devices, per_device(): lax.ppermute(v, ('yh', 'core'), [(0, 1), (1, 2), (2, 3)])  6.21 us
    pallas_call x1, Pallas kernels, spectra_tail(): pl.pallas_call(tail_kernel, in_specs=[pl.BlockSpec(memory_space=pltpu.HBM...  5.16 us
    ppermute x1, waiting for transfers between devices, per_device(): other = lax.ppermute(own, 'core', [(0, 1), (1, 0)])  3.92 us
    ppermute x1, starting transfers between devices, per_device(): other = lax.ppermute(own, 'core', [(0, 1), (1, 0)])  2.49 us
  transfers between devices with their start and end apart: 2, of which 1 were waited for; matrix products, arithmetic and copies ran while one was open for 0% of the time, Pallas kernels for 13%

profile of v3, /device:TPU:1, one launch (start us, length us, event | category | flops | bytes accessed | tf_op | source)
XLA Modules:
  0.0 72.6 jit_solution(15381099669575284138)
XLA Ops:
  0.0 5.2 %spectra_tail.1 = (bf16[16,64,256]{2,1,0:T(8,128)(2,1)S(1)}, bf16[8,32,8,2048]{3,2,1,0:T(8,128)(2,1)S(1)}, f32[16,2048]{1,0:T(8,128)S(1)}, bf16[2048,256]{1,0:T(8,128)(2,1)S(1)}) custom-call(bf16[8,32,8,2048]{3,2,1,0:T(8,128)(2,1)} %bitcast.9, f32[16,2048]{1,0:T(8,128)} %w_ref.1, bf16[2048,256]{1,0:T(8,128)(2,1)} %constant.15.d_ref), custom_call_target="tpu_custom_call" | custom-call | flops 600000000 | bytes 9437184 | tf_op jit(solution)/shard_map/spectra_tail/pallas_call | solution.py:184
  5.2 6.2 %collective-permute-start = (bf16[16,64,256]{2,1,0:T(8,128)(2,1)S(1)}, bf16[16,64,256]{2,1,0:T(8,128)(2,1)S(1)}, u32[]{:S(2)}, u32[]{:S(2)}) collective-permute-start(bf16[16,64,256]{2,1,0:T(8,128)(2,1)S(1)} %get-tuple-element.15), channel_id=1, source_target_pairs={{0,32},{32,64},{64,96},{1,33},{33,65},{65,97},{2,34},{34,66},{66,9... | collective-permute-start | bytes 1572872 | tf_op jit(solution)/shard_map/ppermute | solution.py:362
  11.4 9.4 %spectra_main.1 = (bf16[2,32,2,64,128]{4,3,2,1,0:T(8,128)(2,1)S(1)}, f32[16,64,256]{2,1,0:T(8,128)S(1)}) custom-call(bf16[8,32,8,2048]{3,2,1,0:T(8,128)(2,1)S(1)} %get-tuple-element.11.x_ref, f32[16,2048]{1,0:T(8,128)S(1)} %get-tuple-element.12.w_ref, bf16[2048,256]{1,0:T(8,128)(2,1)S(1)} %get-tuple-element.13.d_ref), custom_call_target="tpu_custom_call" | custom-call | flops 2600000000 | bytes 12582912 | tf_op jit(solution)/shard_map/spectra_main/pallas_call | solution.py:207
  20.7 0.0 collective-permute-done.halo_ref
  20.8 0.5 spectra_join.1
  21.3 36.5 %all_to_all.5 = bf16[64,128,128]{2,1,0:T(8,128)(2,1)S(1)} all-to-all(bf16[64,128,128]{2,1,0:T(8,128)(2,1)S(1)} %bitcast.8), channel_id=1, replica_groups=mesh['yh'=2,'core'=2,'yl'=2,'x'=4,'z'=4] {'yh','yl','x','z'}, dimensions={0} | all-to-all | bytes 4194304 | tf_op jit(solution)/shard_map/all_to_all | solution.py:364
  57.8 2.5 %collective-permute-start.1 = (bf16[64,128,128]{2,1,0:T(8,128)(2,1)S(1)}, bf16[64,128,128]{2,1,0:T(8,128)(2,1)}, u32[]{:S(2)}, u32[]{:S(2)}) collective-permute-start(bf16[64,128,128]{2,1,0:T(8,128)(2,1)S(1)} %all_to_all.5), channel_id=1, source_target_pairs={{0,32},{32,0},{1,33},{33,1},{2,34},{34,2},{3,35},{35,3},{4,36},{36... | collective-permute-start | bytes 6291464 | tf_op jit(solution)/shard_map/ppermute | solution.py:365
  60.3 3.9 %collective-permute-done.1 = bf16[64,128,128]{2,1,0:T(8,128)(2,1)} collective-permute-done((bf16[64,128,128]{2,1,0:T(8,128)(2,1)S(1)}, bf16[64,128,128]{2,1,0:T(8,128)(2,1)}, u32[]{:S(2)}, u32[]{:S(2)}) %collective-permute-start.1) | collective-permute-done | bytes 2097184 | tf_op jit(solution)/shard_map/ppermute | solution.py:365
  64.2 8.3 %correlate.1 = bf16[4,2,512,2048]{3,2,1,0:T(8,128)(2,1)} custom-call(s32[1]{0:T(128)} %bitcast.tm_ref, bf16[64,2,4,16,128]{4,3,2,1,0:T(8,128)(2,1)S(1)} %bitcast.7, bf16[64,2,4,16,128]{4,3,2,1,0:T(8,128)(2,1)} %bitcast.5.other_ref), custom_call_target="tpu_custom_call" | custom-call | flops 4300000256 | bytes 20971520 | tf_op jit(solution)/shard_map/correlate/pallas_call | solution.py:326
Async XLA Ops:
  5.2 15.6 %collective-permute-start = (bf16[16,64,256]{2,1,0:T(8,128)(2,1)S(1)}, bf16[16,64,256]{2,1,0:T(8,128)(2,1)S(1)}, u32[]{:S(2)}, u32[]{:S(2)}) collective-permute-start(bf16[16,64,256]{2,1,0:T(8,128)(2,1)S(1)} %get-tuple-element.15), channel_id=1, source_target_pairs={{0,32},{32,64},{64,96},{1,33},{33,65},{65,97},{2,34},{34,66},{66,9... | collective-permute-start | bytes 1572872 | tf_op jit(solution)/shard_map/ppermute | solution.py:362
  57.8 6.4 %collective-permute-start.1 = (bf16[64,128,128]{2,1,0:T(8,128)(2,1)S(1)}, bf16[64,128,128]{2,1,0:T(8,128)(2,1)}, u32[]{:S(2)}, u32[]{:S(2)}) collective-permute-start(bf16[64,128,128]{2,1,0:T(8,128)(2,1)S(1)} %all_to_all.5), channel_id=1, source_target_pairs={{0,32},{32,0},{1,33},{33,1},{2,34},{34,2},{3,35},{35,3},{4,36},{36... | collective-permute-start | bytes 6291464 | tf_op jit(solution)/shard_map/ppermute | solution.py:365

commit v4 on v3

--- a/solution.py
+++ b/solution.py
@@ -64,9 +64,9 @@
 
 def accumulate(first_in, count_in, first_out, count_out, i, x_ref, w_ref, filt_ref):
     for n in range(0, NT, LANES):
-        at = slice(i * NT + n, i * NT + n + LANES)
+        lanes = slice(n, n + LANES)
         weights = [
-            jnp.broadcast_to(w_ref[p : p + 1, at], (8, LANES)).astype(jnp.bfloat16)
+            jnp.broadcast_to(w_ref[i, p : p + 1, lanes], (8, LANES)).astype(jnp.bfloat16)
             for p in range(TAPS)
         ]
         filtered(
@@ -74,20 +74,21 @@
             count_in,
             first_out,
             count_out,
-            lambda s, f: x_ref[s, f, :, at],
+            lambda s, f: x_ref[i, s, f, :, lanes],
             weights,
             filt_ref,
-            slice(n, n + LANES),
+            lanes,
         )
 
 
 def project(i, count_out, d_ref, filt_ref, acc_ref):
-    table = d_ref[i * NT : i * NT + NT, :]
-    for k in range(0, count_out, 4):
+    table = d_ref[i]
+    step = min(8, count_out)
+    for k in range(0, count_out, step):
         part = jnp.dot(
-            filt_ref[k : k + 4].reshape(4 * SIG, NT), table, preferred_element_type=jnp.float32
+            filt_ref[k : k + step].reshape(step * SIG, NT), table, preferred_element_type=jnp.float32
         )
-        acc_ref[k : k + 4] += part.reshape(4, SIG, COLS)
+        acc_ref[k : k + step] += part.reshape(step, SIG, COLS)
 
 
 def tail_kernel(
@@ -99,18 +100,25 @@
         at = slice(i * NT, i * NT + NT)
         return pltpu.make_async_copy(
             x_ref.at[:, first : first + HALF, :, at],
-            x_out.at[:, first : first + HALF, :, at],
+            x_out.at[i, :, first : first + HALF],
             sems.at[i],
         )
 
-    w_copy = pltpu.make_async_copy(w_ref, w_out, sem.at[slabs])
-    d_copy = pltpu.make_async_copy(d_ref, d_out, sem.at[slabs + 1])
-    w_copy.start()
+    w_copies = [
+        pltpu.make_async_copy(
+            w_ref.at[:, slice(i * NT, i * NT + NT)], w_out.at[i], sem.at[slabs + 1 + i]
+        )
+        for i in range(slabs)
+    ]
+    d_copy = pltpu.make_async_copy(d_ref, d_out, sem.at[slabs])
+    for w_copy in w_copies:
+        w_copy.start()
     copy(HALF, 0, sem).start()
     copy(HALF, 1, sem).start()
     d_copy.start()
     acc_ref[...] = jnp.zeros_like(acc_ref)
-    w_copy.wait()
+    for w_copy in w_copies:
+        w_copy.wait()
 
     for i in range(slabs):
         copy(HALF, i, sem).wait()
@@ -134,19 +142,18 @@
 
 
 def main_kernel(x_ref, w_ref, d_ref, o_ref, early_ref, filt_ref, acc_ref, turn_ref):
-    @pl.when(pl.program_id(0) == 0)
-    def _():
-        acc_ref[...] = jnp.zeros_like(acc_ref)
-
-    accumulate(0, FRAMES, 0, FRAMES, 0, x_ref, w_ref, filt_ref)
-    project(0, FRAMES, d_ref, filt_ref, acc_ref)
-
-    @pl.when(pl.program_id(0) == pl.num_programs(0) - 1)
-    def _():
-        early_ref[...] = acc_ref[:HALF]
-        late = emit(lambda k: acc_ref[HALF + k : HALF + k + 2], turn_ref)
-        o_ref[0, :, 0] = late
-        o_ref[1, :, 0] = late
+    acc_ref[...] = jnp.zeros_like(acc_ref)
+
+    def slab(i, carry):
+        accumulate(0, FRAMES, 0, FRAMES, i, x_ref, w_ref, filt_ref)
+        project(i, FRAMES, d_ref, filt_ref, acc_ref)
+        return carry
+
+    lax.fori_loop(0, NFFT // NT, slab, 0, unroll=2)
+    early_ref[...] = acc_ref[:HALF]
+    late = emit(lambda k: acc_ref[HALF + k : HALF + k + 2], turn_ref)
+    o_ref[0, :, 1] = late
+    o_ref[1, :, 1] = late
 
 
 def join_kernel(early_ref, halo_ref, late_ref, o_ref, turn_ref):
@@ -187,14 +194,14 @@
         out_specs=[VMEM] * 4,
         out_shape=[
             jax.ShapeDtypeStruct((HALF, SIG, COLS), jnp.bfloat16),
-            jax.ShapeDtypeStruct(x4.shape, x4.dtype),
-            jax.ShapeDtypeStruct(taps.shape, taps.dtype),
+            jax.ShapeDtypeStruct((NFFT // NT,) + x4.shape[:3] + (NT,), x4.dtype),
+            jax.ShapeDtypeStruct((NFFT // NT, TAPS, NT), taps.dtype),
             jax.ShapeDtypeStruct(table.shape, table.dtype),
         ],
         scratch_shapes=[
             filt_shape(HALF),
             acc_shape(HALF),
-            pltpu.SemaphoreType.DMA((NFFT // NT + 2,)),
+            pltpu.SemaphoreType.DMA((2 * NFFT // NT + 1,)),
             pltpu.SemaphoreType.DMA((NFFT // NT,)),
         ],
         compiler_params=params(TAIL_MIB),
@@ -203,19 +210,11 @@
     )(x4, taps, table)
 
 
-def spectra_main(x4, taps, table):
+def spectra_main(x, taps, table):
     return pl.pallas_call(
         main_kernel,
-        grid=(NFFT // NT,),
-        in_specs=[
-            pl.BlockSpec((SIG // 8, FRAMES, 8, NT), lambda i: (0, 0, 0, i)),
-            pl.BlockSpec((TAPS, NT), lambda i: (0, i)),
-            pl.BlockSpec((NT, COLS), lambda i: (i, 0)),
-        ],
-        out_specs=[
-            pl.BlockSpec((2, GROUPS, 1, 64, 128), lambda i: (0, 0, 1, 0, 0)),
-            pl.BlockSpec((HALF, SIG, COLS), lambda i: (0, 0, 0)),
-        ],
+        in_specs=[VMEM] * 3,
+        out_specs=[VMEM] * 2,
         out_shape=[
             jax.ShapeDtypeStruct(VOLT_SHAPE, jnp.bfloat16),
             jax.ShapeDtypeStruct((HALF, SIG, COLS), jnp.float32),
@@ -224,7 +223,7 @@
         compiler_params=params(MAIN_MIB),
         cost_estimate=pl.CostEstimate(flops=2_600_000_000, bytes_accessed=12 * MIB, transcendentals=0),
         name="spectra_main",
-    )(x4, taps, table)
+    )(x, taps, table)
 
 
 def spectra_join(early, halo, late):
@@ -348,7 +347,10 @@
 
 def front(samples, tap_weights, send):
     x4 = samples.reshape(SIG // 8, 8, FRAMES, NFFT).transpose(0, 2, 1, 3)
-    operands = [pltpu.with_memory_space_constraint(v, pltpu.HBM) for v in (x4, tap_weights, dft_columns())]
+    table = dft_columns().reshape(NFFT // NT, NT, COLS)
+    operands = [
+        pltpu.with_memory_space_constraint(v, pltpu.HBM) for v in (x4, tap_weights, table)
+    ]
     tail, *held = spectra_tail(*operands)
     halo = send(tail)
     late, early = spectra_main(*held)

time: 72.8 us -> 71.3 us (0.979)
  Pallas kernels: 23.3 us -> 21.8 us
  starting transfers between devices: 8.7 us -> 9.96 us
  blocking collectives: 36.5 us -> 35.3 us
    pallas_call x1, Pallas kernels: 9.35 us -> 7.78 us  [spectra_main(): pl.pallas_call(main_kernel, in_specs=[VMEM] * 3, out_specs=[VMEM] * 2, ou...]
    ppermute x1, starting transfers between devices: 2.49 us -> 3.74 us  [per_device(): other = lax.ppermute(own, 'core', [(0, 1), (1, 0)])]
    all_to_all x1, blocking collectives: 36.5 us -> 35.3 us  [per_device(): own = lax.all_to_all(volts, PEERS, split_axis=0, concat_axis=0, tiled=True)]
  transfers between devices with their start and end apart: 2 -> 2, of which waited for: 1 -> 1; matrix products, arithmetic and copies ran while one was open for 0% -> 0% of each run, Pallas kernels for 13% -> 11%
where the time goes in v4:
time: 71.3 us; the launch traced here: 71.1 us
  blocking collectives  35.3 us (50%)
  Pallas kernels  21.8 us (31%)
  starting transfers between devices  9.96 us (14%)
  waiting for transfers between devices  3.92 us (5%)
    all_to_all x1, blocking collectives, per_device(): own = lax.all_to_all(volts, PEERS, split_axis=0, concat_axis=0, tiled=True)  35.3 us
    pallas_call x1, Pallas kernels, correlate(): pl.pallas_call(functools.partial(correlate_kernel, 1.0 / frames_all), in_...  8.28 us
    pallas_call x1, Pallas kernels, spectra_main(): pl.pallas_call(main_kernel, in_specs=[VMEM] * 3, out_specs=[VMEM] * 2, ou...  7.78 us
    ppermute x1, starting transfers between devices, per_device(): lax.ppermute(v, ('yh', 'core'), [(0, 1), (1, 2), (2, 3)])  6.21 us
    pallas_call x1, Pallas kernels, spectra_tail(): pl.pallas_call(tail_kernel, in_specs=[pl.BlockSpec(memory_space=pltpu.HBM...  5.18 us
    ppermute x1, waiting for transfers between devices, per_device(): other = lax.ppermute(own, 'core', [(0, 1), (1, 0)])  3.92 us
    ppermute x1, starting transfers between devices, per_device(): other = lax.ppermute(own, 'core', [(0, 1), (1, 0)])  3.74 us
  transfers between devices with their start and end apart: 2, of which 1 were waited for; matrix products, arithmetic and copies ran while one was open for 0% of the time, Pallas kernels for 11%

profile of v4, /device:TPU:1, one launch (start us, length us, event | category | flops | bytes accessed | tf_op | source)
XLA Modules:
  0.0 71.1 jit_solution(13152973548379922539)
XLA Ops:
  0.0 5.2 %spectra_tail.1 = (bf16[16,64,256]{2,1,0:T(8,128)(2,1)S(1)}, bf16[4,8,32,8,512]{4,3,2,1,0:T(8,128)(2,1)S(1)}, f32[4,16,512]{2,1,0:T(8,128)S(1)}, bf16[4,512,256]{2,1,0:T(8,128)(2,1)S(1)}) custom-call(bf16[8,32,8,2048]{3,2,1,0:T(8,128)(2,1)} %bitcast.9, f32[16,2048]{1,0:T(8,128)} %w_ref.1, bf16[4,512,256]{2,1,0:T(8,128)(2,1)} %constant.16.d_ref), custom_call_target="tpu_custom_call" | custom-call | flops 600000000 | bytes 9437184 | tf_op jit(solution)/shard_map/spectra_tail/pallas_call | solution.py:191
  5.2 6.2 %collective-permute-start = (bf16[16,64,256]{2,1,0:T(8,128)(2,1)S(1)}, bf16[16,64,256]{2,1,0:T(8,128)(2,1)S(1)}, u32[]{:S(2)}, u32[]{:S(2)}) collective-permute-start(bf16[16,64,256]{2,1,0:T(8,128)(2,1)S(1)} %get-tuple-element.15), channel_id=1, source_target_pairs={{0,32},{32,64},{64,96},{1,33},{33,65},{65,97},{2,34},{34,66},{66,9... | collective-permute-start | bytes 1572872 | tf_op jit(solution)/shard_map/ppermute | solution.py:364
  11.4 7.8 %spectra_main.1 = (bf16[2,32,2,64,128]{4,3,2,1,0:T(8,128)(2,1)S(1)}, f32[16,64,256]{2,1,0:T(8,128)S(1)}) custom-call(bf16[4,8,32,8,512]{4,3,2,1,0:T(8,128)(2,1)S(1)} %get-tuple-element.11.x_ref, f32[4,16,512]{2,1,0:T(8,128)S(1)} %get-tuple-element.12.w_ref, bf16[4,512,256]{2,1,0:T(8,128)(2,1)S(1)} %get-tuple-element.13.d_ref), custom_call_target="tpu_custom_call" | custom-call | flops 2600000000 | bytes 12582912 | tf_op jit(solution)/shard_map/spectra_main/pallas_call | solution.py:214
  19.2 0.0 collective-permute-done.halo_ref
  19.2 0.5 spectra_join.1
  19.8 35.3 %all_to_all.5 = bf16[64,128,128]{2,1,0:T(8,128)(2,1)S(1)} all-to-all(bf16[64,128,128]{2,1,0:T(8,128)(2,1)S(1)} %bitcast.8), channel_id=1, replica_groups=mesh['yh'=2,'core'=2,'yl'=2,'x'=4,'z'=4] {'yh','yl','x','z'}, dimensions={0} | all-to-all | bytes 4194304 | tf_op jit(solution)/shard_map/all_to_all | solution.py:366
  55.0 3.7 %collective-permute-start.1 = (bf16[64,128,128]{2,1,0:T(8,128)(2,1)S(1)}, bf16[64,128,128]{2,1,0:T(8,128)(2,1)}, u32[]{:S(2)}, u32[]{:S(2)}) collective-permute-start(bf16[64,128,128]{2,1,0:T(8,128)(2,1)S(1)} %all_to_all.5), channel_id=1, source_target_pairs={{0,32},{32,0},{1,33},{33,1},{2,34},{34,2},{3,35},{35,3},{4,36},{36... | collective-permute-start | bytes 6291464 | tf_op jit(solution)/shard_map/ppermute | solution.py:367
  58.8 3.9 %collective-permute-done.1 = bf16[64,128,128]{2,1,0:T(8,128)(2,1)} collective-permute-done((bf16[64,128,128]{2,1,0:T(8,128)(2,1)S(1)}, bf16[64,128,128]{2,1,0:T(8,128)(2,1)}, u32[]{:S(2)}, u32[]{:S(2)}) %collective-permute-start.1) | collective-permute-done | bytes 2097184 | tf_op jit(solution)/shard_map/ppermute | solution.py:367
  62.7 8.3 %correlate.1 = bf16[4,2,512,2048]{3,2,1,0:T(8,128)(2,1)} custom-call(s32[1]{0:T(128)} %bitcast.tm_ref, bf16[64,2,4,16,128]{4,3,2,1,0:T(8,128)(2,1)S(1)} %bitcast.7, bf16[64,2,4,16,128]{4,3,2,1,0:T(8,128)(2,1)} %bitcast.5.other_ref), custom_call_target="tpu_custom_call" | custom-call | flops 4300000256 | bytes 20971520 | tf_op jit(solution)/shard_map/correlate/pallas_call | solution.py:325
Async XLA Ops:
  5.2 14.0 %collective-permute-start = (bf16[16,64,256]{2,1,0:T(8,128)(2,1)S(1)}, bf16[16,64,256]{2,1,0:T(8,128)(2,1)S(1)}, u32[]{:S(2)}, u32[]{:S(2)}) collective-permute-start(bf16[16,64,256]{2,1,0:T(8,128)(2,1)S(1)} %get-tuple-element.15), channel_id=1, source_target_pairs={{0,32},{32,64},{64,96},{1,33},{33,65},{65,97},{2,34},{34,66},{66,9... | collective-permute-start | bytes 1572872 | tf_op jit(solution)/shard_map/ppermute | solution.py:364
  55.0 7.7 %collective-permute-start.1 = (bf16[64,128,128]{2,1,0:T(8,128)(2,1)S(1)}, bf16[64,128,128]{2,1,0:T(8,128)(2,1)}, u32[]{:S(2)}, u32[]{:S(2)}) collective-permute-start(bf16[64,128,128]{2,1,0:T(8,128)(2,1)S(1)} %all_to_all.5), channel_id=1, source_target_pairs={{0,32},{32,0},{1,33},{33,1},{2,34},{34,2},{3,35},{35,3},{4,36},{36... | collective-permute-start | bytes 6291464 | tf_op jit(solution)/shard_map/ppermute | solution.py:367

commit v5 on v4

--- a/solution.py
+++ b/solution.py
@@ -129,7 +129,7 @@
         if i == 0:
             d_copy.wait()
         project(i, HALF, d_out, filt_ref, acc_ref)
-    o_ref[...] = acc_ref[...].astype(o_ref.dtype)
+    o_ref[...] = acc_ref[: HALF - 1].astype(o_ref.dtype)
     for i in range(slabs):
         copy(0, i, early_sem).wait()
 
@@ -160,6 +160,9 @@
     del late_ref
 
     def both(k):
+        if k + 2 == HALF:
+            last = early_ref[k : k + 1] + halo_ref[k : k + 1].astype(jnp.float32)
+            return jnp.concatenate([last, early_ref[k + 1 : k + 2]], axis=0)
         return early_ref[k : k + 2] + halo_ref[k : k + 2].astype(jnp.float32)
 
     early = emit(both, turn_ref)
@@ -193,7 +196,7 @@
         in_specs=[pl.BlockSpec(memory_space=pltpu.HBM)] * 3,
         out_specs=[VMEM] * 4,
         out_shape=[
-            jax.ShapeDtypeStruct((HALF, SIG, COLS), jnp.bfloat16),
+            jax.ShapeDtypeStruct((HALF - 1, SIG, COLS), jnp.bfloat16),
             jax.ShapeDtypeStruct((NFFT // NT,) + x4.shape[:3] + (NT,), x4.dtype),
             jax.ShapeDtypeStruct((NFFT // NT, TAPS, NT), taps.dtype),
             jax.ShapeDtypeStruct(table.shape, table.dtype),

time: 71.3 us -> 71.4 us (level)
  no operation moved by 1% of the time
where the time goes in v5:
time: 71.4 us; the launch traced here: 71.2 us
  blocking collectives  35.2 us (49%)
  Pallas kernels  21.9 us (31%)
  starting transfers between devices  9.97 us (14%)
  waiting for transfers between devices  3.92 us (5%)
    all_to_all x1, blocking collectives, per_device(): own = lax.all_to_all(volts, PEERS, split_axis=0, concat_axis=0, tiled=True)  35.2 us
    pallas_call x1, Pallas kernels, correlate(): pl.pallas_call(functools.partial(correlate_kernel, 1.0 / frames_all), in_...  8.29 us
    pallas_call x1, Pallas kernels, spectra_main(): pl.pallas_call(main_kernel, in_specs=[VMEM] * 3, out_specs=[VMEM] * 2, ou...  7.78 us
    ppermute x1, starting transfers between devices, per_device(): lax.ppermute(v, ('yh', 'core'), [(0, 1), (1, 2), (2, 3)])  6.21 us
    pallas_call x1, Pallas kernels, spectra_tail(): pl.pallas_call(tail_kernel, in_specs=[pl.BlockSpec(memory_space=pltpu.HBM...  5.28 us
    ppermute x1, waiting for transfers between devices, per_device(): other = lax.ppermute(own, 'core', [(0, 1), (1, 0)])  3.92 us
    ppermute x1, starting transfers between devices, per_device(): other = lax.ppermute(own, 'core', [(0, 1), (1, 0)])  3.76 us
  transfers between devices with their start and end apart: 2, of which 1 were waited for; matrix products, arithmetic and copies ran while one was open for 0% of the time, Pallas kernels for 11%

profile of v5, /device:TPU:1, one launch (start us, length us, event | category | flops | bytes accessed | tf_op | source)
XLA Modules:
  0.0 71.2 jit_solution(199164256426083895)
XLA Ops:
  0.0 5.3 %spectra_tail.1 = (bf16[15,64,256]{2,1,0:T(8,128)(2,1)S(1)}, bf16[4,8,32,8,512]{4,3,2,1,0:T(8,128)(2,1)S(1)}, f32[4,16,512]{2,1,0:T(8,128)S(1)}, bf16[4,512,256]{2,1,0:T(8,128)(2,1)S(1)}) custom-call(bf16[8,32,8,2048]{3,2,1,0:T(8,128)(2,1)} %bitcast.9, f32[16,2048]{1,0:T(8,128)} %w_ref.1, bf16[4,512,256]{2,1,0:T(8,128)(2,1)} %constant.16.d_ref), custom_call_target="tpu_custom_call" | custom-call | flops 600000000 | bytes 9437184 | tf_op jit(solution)/shard_map/spectra_tail/pallas_call | solution.py:194
  5.3 6.2 %collective-permute-start = (bf16[15,64,256]{2,1,0:T(8,128)(2,1)S(1)}, bf16[15,64,256]{2,1,0:T(8,128)(2,1)S(1)}, u32[]{:S(2)}, u32[]{:S(2)}) collective-permute-start(bf16[15,64,256]{2,1,0:T(8,128)(2,1)S(1)} %get-tuple-element.15), channel_id=1, source_target_pairs={{0,32},{32,64},{64,96},{1,33},{33,65},{65,97},{2,34},{34,66},{66,9... | collective-permute-start | bytes 1474568 | tf_op jit(solution)/shard_map/ppermute | solution.py:367
  11.5 7.8 %spectra_main.1 = (bf16[2,32,2,64,128]{4,3,2,1,0:T(8,128)(2,1)S(1)}, f32[16,64,256]{2,1,0:T(8,128)S(1)}) custom-call(bf16[4,8,32,8,512]{4,3,2,1,0:T(8,128)(2,1)S(1)} %get-tuple-element.11.x_ref, f32[4,16,512]{2,1,0:T(8,128)S(1)} %get-tuple-element.12.w_ref, bf16[4,512,256]{2,1,0:T(8,128)(2,1)S(1)} %get-tuple-element.13.d_ref), custom_call_target="tpu_custom_call" | custom-call | flops 2600000000 | bytes 12582912 | tf_op jit(solution)/shard_map/spectra_main/pallas_call | solution.py:217
  19.3 0.0 collective-permute-done.halo_ref
  19.3 0.5 spectra_join.1
  19.9 35.2 %all_to_all.5 = bf16[64,128,128]{2,1,0:T(8,128)(2,1)S(1)} all-to-all(bf16[64,128,128]{2,1,0:T(8,128)(2,1)S(1)} %bitcast.8), channel_id=1, replica_groups=mesh['yh'=2,'core'=2,'yl'=2,'x'=4,'z'=4] {'yh','yl','x','z'}, dimensions={0} | all-to-all | bytes 4194304 | tf_op jit(solution)/shard_map/all_to_all | solution.py:369
  55.1 3.8 %collective-permute-start.1 = (bf16[64,128,128]{2,1,0:T(8,128)(2,1)S(1)}, bf16[64,128,128]{2,1,0:T(8,128)(2,1)}, u32[]{:S(2)}, u32[]{:S(2)}) collective-permute-start(bf16[64,128,128]{2,1,0:T(8,128)(2,1)S(1)} %all_to_all.5), channel_id=1, source_target_pairs={{0,32},{32,0},{1,33},{33,1},{2,34},{34,2},{3,35},{35,3},{4,36},{36... | collective-permute-start | bytes 6291464 | tf_op jit(solution)/shard_map/ppermute | solution.py:370
  58.8 3.9 %collective-permute-done.1 = bf16[64,128,128]{2,1,0:T(8,128)(2,1)} collective-permute-done((bf16[64,128,128]{2,1,0:T(8,128)(2,1)S(1)}, bf16[64,128,128]{2,1,0:T(8,128)(2,1)}, u32[]{:S(2)}, u32[]{:S(2)}) %collective-permute-start.1) | collective-permute-done | bytes 2097184 | tf_op jit(solution)/shard_map/ppermute | solution.py:370
  62.8 8.3 %correlate.1 = bf16[4,2,512,2048]{3,2,1,0:T(8,128)(2,1)} custom-call(s32[1]{0:T(128)} %bitcast.tm_ref, bf16[64,2,4,16,128]{4,3,2,1,0:T(8,128)(2,1)S(1)} %bitcast.7, bf16[64,2,4,16,128]{4,3,2,1,0:T(8,128)(2,1)} %bitcast.5.other_ref), custom_call_target="tpu_custom_call" | custom-call | flops 4300000256 | bytes 20971520 | tf_op jit(solution)/shard_map/correlate/pallas_call | solution.py:328
Async XLA Ops:
  5.3 14.0 %collective-permute-start = (bf16[15,64,256]{2,1,0:T(8,128)(2,1)S(1)}, bf16[15,64,256]{2,1,0:T(8,128)(2,1)S(1)}, u32[]{:S(2)}, u32[]{:S(2)}) collective-permute-start(bf16[15,64,256]{2,1,0:T(8,128)(2,1)S(1)} %get-tuple-element.15), channel_id=1, source_target_pairs={{0,32},{32,64},{64,96},{1,33},{33,65},{65,97},{2,34},{34,66},{66,9... | collective-permute-start | bytes 1474568 | tf_op jit(solution)/shard_map/ppermute | solution.py:367
  55.1 7.7 %collective-permute-start.1 = (bf16[64,128,128]{2,1,0:T(8,128)(2,1)S(1)}, bf16[64,128,128]{2,1,0:T(8,128)(2,1)}, u32[]{:S(2)}, u32[]{:S(2)}) collective-permute-start(bf16[64,128,128]{2,1,0:T(8,128)(2,1)S(1)} %all_to_all.5), channel_id=1, source_target_pairs={{0,32},{32,0},{1,33},{33,1},{2,34},{34,2},{3,35},{35,3},{4,36},{36... | collective-permute-start | bytes 6291464 | tf_op jit(solution)/shard_map/ppermute | solution.py:370
